TPU v7x, 32 devices: a whole 2x2x4 slice. The times are simulated.
32 devices in a mesh: gx: 4 (over x, core), yz: 8 (over z, y).
Axes of the slice: x: 2, y: 2, z: 4, core: 2. Of those that a mesh axis runs over, the one named last changes fastest.
Arguments:
- owners: int32 [4096, 1], P(('gx', 'yz')), may hold values from 0 to 31; in each aligned block of 128 rows (0 to 127, 128 to 255, ...) at most 8 rows name the same one
- bricks: int32 [4096], P(('gx', 'yz')), may hold values from 0 to 63
- cells: int32 [4096, 3, 128], P(('gx', 'yz')), may hold values from 0 to 7
- offsets: float32 [4096, 3, 128], P(('gx', 'yz')), may hold values from 0.5 to 1.5
- mass: float32 [4096, 128], P(('gx', 'yz')), may hold values from 0.5 to 2
- velocity: float32 [4096, 3, 128], P(('gx', 'yz')), may hold values from -6 to 6
- affine: float32 [4096, 9, 128], P(('gx', 'yz')), may hold values from -4 to 4
Outputs:
- grid_mass: float32 [64, 128, 128], P('gx', 'yz')
- grid_velocity: float32 [3, 64, 128, 128], P(None, 'gx', 'yz')
Inputs may be any that keep to these rules, and one draw needn't show every extreme that they name: In the owners of each aligned group of 128 rows (the blocks of one device) no device is named more than 8 times, and some device is named exactly 8 times.
All inputs are finite; a program needn't handle non-finite values.
Results may differ from a plain program's by a relative error of at most 0.0003.
Values sent between devices are 32-bit elements; how exact they have to be, the bound alone decides.
A program may use at most 128 MiB of HBM per device.

v0:
```python
import jax
import jax.numpy as jnp
from jax import lax
from jax.sharding import PartitionSpec as P

FACE = 16
CZ = 128


HIGH = lax.Precision.HIGHEST


def passed_along(array, axis, by):
    devices = lax.axis_size(axis)
    pairs = [(i, i + by) for i in range(devices) if 0 <= i + by < devices]
    return lax.ppermute(array, axis, pairs)


def axis_weights(frac, corner):
    spots = jnp.arange(10)[None, :, None]
    first = 0.5 * (1.5 - frac) ** 2
    middle = 0.75 - (frac - 1.0) ** 2
    last = 0.5 * (frac - 0.5) ** 2
    total = first[:, None, :] * (spots == corner[:, None, :]).astype(jnp.float32)
    total = total + middle[:, None, :] * (spots == corner[:, None, :] + 1).astype(jnp.float32)
    return total + last[:, None, :] * (spots == corner[:, None, :] + 2).astype(jnp.float32)


def brick_tile(block):
    count = block.shape[1]
    frac = block[0:3]
    pmass = block[3]
    pvel = block[4:7]
    matrix = block[7:16].reshape(3, 3, count)
    code = block[16].astype(jnp.int32)
    flat_cell = code % 512
    corner = jnp.stack([flat_cell // 64, flat_cell // 8 % 8, flat_cell % 8])
    spread = axis_weights(frac, corner)
    weight = (
        spread[0][:, None, None, :] * spread[1][None, :, None, :] * spread[2][None, None, :, :]
    ).reshape(1000, count)
    place = corner.astype(jnp.float32) + frac
    shifted = pmass[None] * pvel - jnp.einsum("ijp,jp->ip", matrix, place, precision=HIGH)
    columns = jnp.concatenate([pmass[None], shifted, block[7:16]], axis=0)
    return lax.dot_general(
        columns,
        weight,
        (((1,), (1,)), ((), ())),
        precision=HIGH,
        preferred_element_type=jnp.float32,
    )


def lay_last(arr):
    nbk = arr.shape[-2]
    lead = arr.shape[:-2]
    lower = arr[..., 0:8].reshape(lead + (8 * nbk,))
    upper = jnp.concatenate(
        [arr[..., 8:10], jnp.zeros(lead + (nbk, 6), jnp.float32)], axis=-1
    ).reshape(lead + (8 * nbk,))
    pad_low = [(0, 0)] * len(lead) + [(0, 2)]
    pad_up = [(0, 0)] * len(lead) + [(8, 0)]
    return jnp.pad(lower, pad_low) + jnp.pad(upper, pad_up)[..., : 8 * nbk + 2]


def x_rim(rim, by):
    return passed_along(rim, "gx", by)


def y_rim(rim, by):
    return passed_along(rim, "yz", by)


def sum_x(grid):
    edge = grid.shape[1] - 2
    from_below = x_rim(grid[:, edge + 1 : edge + 2], 1)
    from_above = x_rim(grid[:, 0:1], -1)
    return grid.at[:, 1:2].add(from_below).at[:, edge : edge + 1].add(from_above)


def sum_y(grid):
    edge = grid.shape[2] - 2
    from_below = y_rim(grid[:, :, edge + 1 : edge + 2], 1)
    from_above = y_rim(grid[:, :, 0:1], -1)
    return grid.at[:, :, 1:2].add(from_below).at[:, :, edge : edge + 1].add(from_above)


def local(owners, bricks, cells, offsets, mass, velocity, affine):
    nblk, count = mass.shape
    depth = CZ
    side = FACE
    per_side = side // 8
    per_depth = depth // 8
    nbz = per_side * per_side * per_depth
    rows_gx = lax.axis_size("gx")
    rows_yz = lax.axis_size("yz")
    ndev = rows_gx * rows_yz
    cap = 2 * nblk // ndev
    slots = ndev * cap
    width = 17 * count
    dest = owners[:, 0]
    same = (dest[:, None] == dest[None, :]).astype(jnp.int32)
    order = jnp.arange(nblk)
    before = (order[:, None] < order[None, :]).astype(jnp.int32)
    rank = jnp.sum(same * before, axis=0)
    target = dest * cap + rank
    select = (jnp.arange(slots)[:, None] == target[None, :]).astype(jnp.float32)
    flat_cell = cells[:, 0] * 64 + cells[:, 1] * 8 + cells[:, 2]
    code = (bricks[:, None] * 512 + flat_cell).astype(jnp.float32)
    payload = jnp.concatenate([offsets, mass[:, None], velocity, affine, code[:, None]], axis=1)
    packed = jnp.dot(
        select, payload.reshape(nblk, width), precision=HIGH, preferred_element_type=jnp.float32
    )
    moved = lax.all_to_all(packed, ("gx", "yz"), split_axis=0, concat_axis=0, tiled=True)
    received = moved.reshape(slots, 17, count)
    groups = received.reshape(slots // 16, 16, 17, count)
    tiles = lax.map(jax.vmap(brick_tile), groups).reshape(slots, 13, 1000)
    brick_of = received[:, 16, 0].astype(jnp.int32) // 512
    pick = (brick_of[:, None] == jnp.arange(nbz)[None, :]).astype(jnp.float32)
    sums = jnp.einsum("sb,scn->bcn", pick, tiles, precision=HIGH)
    node = jnp.arange(1000)
    coord = jnp.stack([node // 100, node // 10 % 10, node % 10]).astype(jnp.float32)
    moment = sums[:, 1:4] + jnp.einsum(
        "bijn,jn->bin", sums[:, 4:13].reshape(nbz, 3, 3, 1000), coord, precision=HIGH
    )
    nodal = jnp.concatenate([sums[:, 0:1], moment], axis=1).reshape(
        per_side, per_side, per_depth, 4, 10, 10, 10
    )
    along_z = lay_last(jnp.transpose(nodal, (3, 0, 1, 4, 5, 2, 6)))
    along_y = lay_last(jnp.transpose(along_z, (0, 1, 3, 5, 2, 4)))
    along_x = lay_last(jnp.transpose(along_y, (0, 3, 4, 1, 2)))
    grid = jnp.transpose(along_x, (0, 3, 2, 1))
    grid = sum_y(sum_x(grid))
    inner = grid[:, 1 : side + 1, 1 : side + 1, 1 : depth + 1]
    node_mass = inner[0]
    speed = inner[1:4] / jnp.maximum(node_mass, 0.5)[None]
    speed = speed + jnp.array([0.0, 0.0, -0.5], jnp.float32)[:, None, None, None]
    index_x = lax.axis_index("gx") * side + jnp.arange(side)
    index_y = lax.axis_index("yz") * side + jnp.arange(side)
    index_z = jnp.arange(depth)
    inside_x = (index_x > 0) & (index_x < side * rows_gx - 1)
    inside_y = (index_y > 0) & (index_y < side * rows_yz - 1)
    inside_z = (index_z > 0) & (index_z < depth - 1)
    inside = inside_x[:, None, None] & inside_y[None, :, None] & inside_z[None, None, :]
    speed = jnp.where(inside[None], speed, 0.0)
    return (node_mass, speed)


def solution(mesh):
    return jax.shard_map(
        local,
        mesh=mesh,
        in_specs=(
            P(("gx", "yz"), None),
            P(("gx", "yz")),
            P(("gx", "yz"), None, None),
            P(("gx", "yz"), None, None),
            P(("gx", "yz"), None),
            P(("gx", "yz"), None, None),
            P(("gx", "yz"), None, None),
        ),
        out_specs=(P("gx", "yz", None), P(None, "gx", "yz", None)),
        check_vma=False,
    )
```

profile of v0, /device:TPU:5, one launch (start us, length us, event | category | flops | bytes accessed | tf_op | source)
XLA Modules:
  0.0 421.6 jit_solution(13702830638928417049)
XLA Ops:
  7.5 2.5 fusion.24
  10.0 6.4 %all-to-all-start = ((f32[32,8,2176]{2,1,0:T(8,128)}), f32[32,8,2176]{2,1,0:T(8,128)S(1)}, u32[]{:S(2)}, u32[]{:S(2)}) async-start(f32[32,8,2176]{2,1,0:T(8,128)} %fusion.24), calls=%async_computation | async-start | bytes 4456448 | tf_op jit(solution)/shard_map/all_to_all | solution.py:114
  16.5 51.7 %all-to-all-done = f32[32,8,2176]{2,1,0:T(8,128)S(1)} async-done(((f32[32,8,2176]{2,1,0:T(8,128)}), f32[32,8,2176]{2,1,0:T(8,128)S(1)}, u32[]{:S(2)}, u32[]{:S(2)}) %all-to-all-start) | async-done | bytes 2228256 | tf_op jit(solution)/shard_map/all_to_all | solution.py:114
  70.0 3.7 copy.154
  75.5 5.8 %fusion.23 = s32[256]{0:T(256)S(1)} fusion(f32[256,17,128]{2,1,0:T(8,128)} %reshape.605), kind=kLoop, calls=%fused_computation.66 | loop fusion | flops 256 | bytes 2048 | tf_op jit(solution)/shard_map/convert_element_type | solution.py:118
  81.3 214.9 %while.17 = (s32[]{:T(128)}, f32[16,16,13,1000]{3,2,1,0:T(8,128)}, f32[16,16,17,128]{3,1,2,0:T(8,128)}, s32[]{:T(128)}) while((s32[]{:T(128)}, f32[16,16,13,1000]{3,2,1,0:T(8,128)}, f32[16,16,17,128]{3,1,2,0:T(8,128)}, s32[]{:T(128)}) %tuple.77), condition=%wide.region_2.3_spmd, body=%wide.region_1.2_spmd.sunk | while | flops 322551808 | bytes 21504068 | solution.py:117
  84.3 10.9 %fusion.54 = f32[16,16,13,1000]{3,2,1,0:T(8,128)} fusion(f32[16,16,13,1000]{3,2,1,0:T(8,128)} %get-tuple-element.218, s32[]{:T(128)S(6)} %copy.212, f32[16,1000,128]{2,0,1:T(8,128)S(1)} %bitcast.118, f32[16,13,128]{2,0,1:T(8,128)S(1)} %pad_maximum_fusion.3), kind=kOutput, calls=%fused_computation.4.clone.1 | convolution fusion | flops 319488000 | bytes 9347076 | tf_op jit(solution)/shard_map/while/body/eval_jaxpr/vmap()/dot_general | solution.py:45
  97.7 11.0 %fusion.54 = f32[16,16,13,1000]{3,2,1,0:T(8,128)} fusion(f32[16,16,13,1000]{3,2,1,0:T(8,128)} %get-tuple-element.218, s32[]{:T(128)S(6)} %copy.212, f32[16,1000,128]{2,0,1:T(8,128)S(1)} %bitcast.118, f32[16,13,128]{2,0,1:T(8,128)S(1)} %pad_maximum_fusion.3), kind=kOutput, calls=%fused_computation.4.clone.1 | convolution fusion | flops 319488000 | bytes 9347076 | tf_op jit(solution)/shard_map/while/body/eval_jaxpr/vmap()/dot_general | solution.py:45
  111.1 10.9 %fusion.54 = f32[16,16,13,1000]{3,2,1,0:T(8,128)} fusion(f32[16,16,13,1000]{3,2,1,0:T(8,128)} %get-tuple-element.218, s32[]{:T(128)S(6)} %copy.212, f32[16,1000,128]{2,0,1:T(8,128)S(1)} %bitcast.118, f32[16,13,128]{2,0,1:T(8,128)S(1)} %pad_maximum_fusion.3), kind=kOutput, calls=%fused_computation.4.clone.1 | convolution fusion | flops 319488000 | bytes 9347076 | tf_op jit(solution)/shard_map/while/body/eval_jaxpr/vmap()/dot_general | solution.py:45
  124.5 10.9 %fusion.54 = f32[16,16,13,1000]{3,2,1,0:T(8,128)} fusion(f32[16,16,13,1000]{3,2,1,0:T(8,128)} %get-tuple-element.218, s32[]{:T(128)S(6)} %copy.212, f32[16,1000,128]{2,0,1:T(8,128)S(1)} %bitcast.118, f32[16,13,128]{2,0,1:T(8,128)S(1)} %pad_maximum_fusion.3), kind=kOutput, calls=%fused_computation.4.clone.1 | convolution fusion | flops 319488000 | bytes 9347076 | tf_op jit(solution)/shard_map/while/body/eval_jaxpr/vmap()/dot_general | solution.py:45
  137.9 10.9 %fusion.54 = f32[16,16,13,1000]{3,2,1,0:T(8,128)} fusion(f32[16,16,13,1000]{3,2,1,0:T(8,128)} %get-tuple-element.218, s32[]{:T(128)S(6)} %copy.212, f32[16,1000,128]{2,0,1:T(8,128)S(1)} %bitcast.118, f32[16,13,128]{2,0,1:T(8,128)S(1)} %pad_maximum_fusion.3), kind=kOutput, calls=%fused_computation.4.clone.1 | convolution fusion | flops 319488000 | bytes 9347076 | tf_op jit(solution)/shard_map/while/body/eval_jaxpr/vmap()/dot_general | solution.py:45
  151.3 11.0 %fusion.54 = f32[16,16,13,1000]{3,2,1,0:T(8,128)} fusion(f32[16,16,13,1000]{3,2,1,0:T(8,128)} %get-tuple-element.218, s32[]{:T(128)S(6)} %copy.212, f32[16,1000,128]{2,0,1:T(8,128)S(1)} %bitcast.118, f32[16,13,128]{2,0,1:T(8,128)S(1)} %pad_maximum_fusion.3), kind=kOutput, calls=%fused_computation.4.clone.1 | convolution fusion | flops 319488000 | bytes 9347076 | tf_op jit(solution)/shard_map/while/body/eval_jaxpr/vmap()/dot_general | solution.py:45
  164.7 10.9 %fusion.54 = f32[16,16,13,1000]{3,2,1,0:T(8,128)} fusion(f32[16,16,13,1000]{3,2,1,0:T(8,128)} %get-tuple-element.218, s32[]{:T(128)S(6)} %copy.212, f32[16,1000,128]{2,0,1:T(8,128)S(1)} %bitcast.118, f32[16,13,128]{2,0,1:T(8,128)S(1)} %pad_maximum_fusion.3), kind=kOutput, calls=%fused_computation.4.clone.1 | convolution fusion | flops 319488000 | bytes 9347076 | tf_op jit(solution)/shard_map/while/body/eval_jaxpr/vmap()/dot_general | solution.py:45
  178.1 11.0 %fusion.54 = f32[16,16,13,1000]{3,2,1,0:T(8,128)} fusion(f32[16,16,13,1000]{3,2,1,0:T(8,128)} %get-tuple-element.218, s32[]{:T(128)S(6)} %copy.212, f32[16,1000,128]{2,0,1:T(8,128)S(1)} %bitcast.118, f32[16,13,128]{2,0,1:T(8,128)S(1)} %pad_maximum_fusion.3), kind=kOutput, calls=%fused_computation.4.clone.1 | convolution fusion | flops 319488000 | bytes 9347076 | tf_op jit(solution)/shard_map/while/body/eval_jaxpr/vmap()/dot_general | solution.py:45
  191.5 11.0 %fusion.54 = f32[16,16,13,1000]{3,2,1,0:T(8,128)} fusion(f32[16,16,13,1000]{3,2,1,0:T(8,128)} %get-tuple-element.218, s32[]{:T(128)S(6)} %copy.212, f32[16,1000,128]{2,0,1:T(8,128)S(1)} %bitcast.118, f32[16,13,128]{2,0,1:T(8,128)S(1)} %pad_maximum_fusion.3), kind=kOutput, calls=%fused_computation.4.clone.1 | convolution fusion | flops 319488000 | bytes 9347076 | tf_op jit(solution)/shard_map/while/body/eval_jaxpr/vmap()/dot_general | solution.py:45
  204.9 10.9 %fusion.54 = f32[16,16,13,1000]{3,2,1,0:T(8,128)} fusion(f32[16,16,13,1000]{3,2,1,0:T(8,128)} %get-tuple-element.218, s32[]{:T(128)S(6)} %copy.212, f32[16,1000,128]{2,0,1:T(8,128)S(1)} %bitcast.118, f32[16,13,128]{2,0,1:T(8,128)S(1)} %pad_maximum_fusion.3), kind=kOutput, calls=%fused_computation.4.clone.1 | convolution fusion | flops 319488000 | bytes 9347076 | tf_op jit(solution)/shard_map/while/body/eval_jaxpr/vmap()/dot_general | solution.py:45
  218.3 10.9 %fusion.54 = f32[16,16,13,1000]{3,2,1,0:T(8,128)} fusion(f32[16,16,13,1000]{3,2,1,0:T(8,128)} %get-tuple-element.218, s32[]{:T(128)S(6)} %copy.212, f32[16,1000,128]{2,0,1:T(8,128)S(1)} %bitcast.118, f32[16,13,128]{2,0,1:T(8,128)S(1)} %pad_maximum_fusion.3), kind=kOutput, calls=%fused_computation.4.clone.1 | convolution fusion | flops 319488000 | bytes 9347076 | tf_op jit(solution)/shard_map/while/body/eval_jaxpr/vmap()/dot_general | solution.py:45
  231.7 10.9 %fusion.54 = f32[16,16,13,1000]{3,2,1,0:T(8,128)} fusion(f32[16,16,13,1000]{3,2,1,0:T(8,128)} %get-tuple-element.218, s32[]{:T(128)S(6)} %copy.212, f32[16,1000,128]{2,0,1:T(8,128)S(1)} %bitcast.118, f32[16,13,128]{2,0,1:T(8,128)S(1)} %pad_maximum_fusion.3), kind=kOutput, calls=%fused_computation.4.clone.1 | convolution fusion | flops 319488000 | bytes 9347076 | tf_op jit(solution)/shard_map/while/body/eval_jaxpr/vmap()/dot_general | solution.py:45
  245.1 11.0 %fusion.54 = f32[16,16,13,1000]{3,2,1,0:T(8,128)} fusion(f32[16,16,13,1000]{3,2,1,0:T(8,128)} %get-tuple-element.218, s32[]{:T(128)S(6)} %copy.212, f32[16,1000,128]{2,0,1:T(8,128)S(1)} %bitcast.118, f32[16,13,128]{2,0,1:T(8,128)S(1)} %pad_maximum_fusion.3), kind=kOutput, calls=%fused_computation.4.clone.1 | convolution fusion | flops 319488000 | bytes 9347076 | tf_op jit(solution)/shard_map/while/body/eval_jaxpr/vmap()/dot_general | solution.py:45
  258.5 10.9 %fusion.54 = f32[16,16,13,1000]{3,2,1,0:T(8,128)} fusion(f32[16,16,13,1000]{3,2,1,0:T(8,128)} %get-tuple-element.218, s32[]{:T(128)S(6)} %copy.212, f32[16,1000,128]{2,0,1:T(8,128)S(1)} %bitcast.118, f32[16,13,128]{2,0,1:T(8,128)S(1)} %pad_maximum_fusion.3), kind=kOutput, calls=%fused_computation.4.clone.1 | convolution fusion | flops 319488000 | bytes 9347076 | tf_op jit(solution)/shard_map/while/body/eval_jaxpr/vmap()/dot_general | solution.py:45
  271.9 10.9 %fusion.54 = f32[16,16,13,1000]{3,2,1,0:T(8,128)} fusion(f32[16,16,13,1000]{3,2,1,0:T(8,128)} %get-tuple-element.218, s32[]{:T(128)S(6)} %copy.212, f32[16,1000,128]{2,0,1:T(8,128)S(1)} %bitcast.118, f32[16,13,128]{2,0,1:T(8,128)S(1)} %pad_maximum_fusion.3), kind=kOutput, calls=%fused_computation.4.clone.1 | convolution fusion | flops 319488000 | bytes 9347076 | tf_op jit(solution)/shard_map/while/body/eval_jaxpr/vmap()/dot_general | solution.py:45
  285.3 10.9 %fusion.54 = f32[16,16,13,1000]{3,2,1,0:T(8,128)} fusion(f32[16,16,13,1000]{3,2,1,0:T(8,128)} %get-tuple-element.218, s32[]{:T(128)S(6)} %copy.212, f32[16,1000,128]{2,0,1:T(8,128)S(1)} %bitcast.118, f32[16,13,128]{2,0,1:T(8,128)S(1)} %pad_maximum_fusion.3), kind=kOutput, calls=%fused_computation.4.clone.1 | convolution fusion | flops 319488000 | bytes 9347076 | tf_op jit(solution)/shard_map/while/body/eval_jaxpr/vmap()/dot_general | solution.py:45
  296.2 18.9 %fusion.18 = f32[64,13,1000]{2,0,1:T(8,128)S(1)} fusion(f32[256,13,1000]{2,1,0:T(8,128)} %bitcast.122, s32[256]{0:T(256)S(1)} %and_select_fusion.4), kind=kOutput, calls=%fused_computation.51 | convolution fusion | flops 2555920384 | bytes 16641024 | tf_op jit(solution)/shard_map/sb,scn->bcn/dot_general | solution.py:120
  316.5 8.1 %reshape.608 = f32[2,2,16,4,10,10,10]{2,1,0,6,5,4,3:T(2,128)} reshape(f32[64,4,1000]{0,2,1:T(8,128)S(1)} %copy.156) | data formatting | bytes 2048000 | tf_op jit(solution)/shard_map/reshape | solution.py:126
  326.7 11.0 %slice.280 = f32[4,2,2,10,10,16,8]{5,2,1,6,4,3,0:T(2,128)} slice(f32[4,2,2,10,10,16,10]{5,2,1,6,4,3,0:T(2,128)} %bitcast.120), slice={[0:4], [0:2], [0:2], [0:10], [0:10], [0:16], [0:8]} | slice | bytes 1638400 | tf_op jit(solution)/shard_map/slice | solution.py:57
  337.6 13.9 %copy.157 = f32[4,2,2,10,10,16,8]{6,5,2,4,3,1,0:T(8,128)} copy(f32[4,2,2,10,10,16,8]{5,2,1,6,4,3,0:T(2,128)} %slice.280) | data formatting | bytes 1638400 | tf_op jit(solution)/shard_map/slice | solution.py:57
  351.6 9.8 %reshape.609 = f32[4,2,2,10,10,128]{5,2,4,3,1,0:T(2,128)S(1)} reshape(f32[4,2,2,10,10,16,8]{6,5,2,4,3,1,0:T(8,128)} %copy.157) | data formatting | bytes 1638400 | tf_op jit(solution)/shard_map/reshape | solution.py:57
  361.4 11.7 %copy.185 = f32[4,2,2,10,10,16,2]{6,5,2,4,3,1,0:T(8,128)} copy(f32[4,2,2,10,10,16,2]{5,2,1,6,4,3,0:T(2,128)S(1)} %slice.281) | data formatting | bytes 409600
  373.1 12.5 %concatenate.32.clone = f32[4,2,2,10,10,16,8]{6,5,2,4,3,1,0:T(8,128)} pad(f32[4,2,2,10,10,16,2]{6,5,2,4,3,1,0:T(8,128)} %copy.185, f32[]{:T(128)} %constant.328.clone.1), padding=0_0x0_0x0_0x0_0x0_0x0_0x0_6 | pad | bytes 1024004 | tf_op jit(solution)/shard_map/concatenate | solution.py:58
  385.5 10.1 %reshape.610 = f32[4,2,2,10,10,128]{5,2,4,3,1,0:T(2,128)S(1)} reshape(f32[4,2,2,10,10,16,8]{6,5,2,4,3,1,0:T(8,128)} %concatenate.32.clone) | data formatting | bytes 1638400 | tf_op jit(solution)/shard_map/reshape | solution.py:60
  405.4 4.7 %collective-permute-done.1 = f32[4,1,18,130]{3,2,1,0:T(8,128)S(1)} collective-permute-done((f32[4,1,18,130]{3,2,1,0:T(8,128)S(1)}, f32[4,1,18,130]{3,2,1,0:T(8,128)S(1)}, u32[]{:S(2)}, u32[]{:S(2)}) %collective-permute-start.1) | collective-permute-done | bytes 37472 | tf_op jit(solution)/shard_map/ppermute | solution.py:16
  412.3 3.4 collective-permute-start.3
  (293 shorter events, 69.0 us)
Async XLA Ops:
  0.6 6.5 %copy-start = (f32[128,9,128]{2,0,1:T(8,128)S(1)}, f32[128,9,128]{2,0,1:T(8,128)}, u32[]{:S(2)}) copy-start(f32[128,9,128]{2,0,1:T(8,128)} %param.24) | copy-start | bytes 1769476
  10.0 58.2 %all-to-all-start = ((f32[32,8,2176]{2,1,0:T(8,128)}), f32[32,8,2176]{2,1,0:T(8,128)S(1)}, u32[]{:S(2)}, u32[]{:S(2)}) async-start(f32[32,8,2176]{2,1,0:T(8,128)} %fusion.24), calls=%async_computation | async-start | bytes 4456448 | tf_op jit(solution)/shard_map/all_to_all | solution.py:114
  399.5 3.9 collective-permute-start
  402.0 18.4 %copy-start.1 = (f32[3]{0:T(128)S(1)}, f32[3]{0:T(128)}, u32[]{:S(2)}) copy-start(f32[3]{0:T(128)} %constant.337.clone) | copy-start | bytes 40
  403.5 6.6 %collective-permute-start.1 = (f32[4,1,18,130]{3,2,1,0:T(8,128)S(1)}, f32[4,1,18,130]{3,2,1,0:T(8,128)S(1)}, u32[]{:S(2)}, u32[]{:S(2)}) collective-permute-start(f32[4,1,18,130]{3,2,1,0:T(8,128)S(1)} %get-tuple-element.157), channel_id=1, source_target_pairs={{8,0},{16,8},{24,16},{9,1},{17,9},{25,17},{10,2},{18,10},{26,18},{... | collective-permute-start | bytes 112328 | tf_op jit(solution)/shard_map/ppermute | solution.py:16
  410.3 6.4 %collective-permute-start.2 = (f32[4,18,1,130]{3,1,2,0:T(8,128)S(1)}, f32[4,18,1,130]{3,1,2,0:T(8,128)S(1)}, u32[]{:S(2)}, u32[]{:S(2)}) collective-permute-start(f32[4,18,1,130]{3,1,2,0:T(8,128)S(1)} %copy.161), channel_id=1, source_target_pairs={{0,1},{1,2},{2,3},{3,4},{4,5},{5,6},{6,7},{8,9},{9,10},{10,11},{11... | collective-permute-start | bytes 112328 | tf_op jit(solution)/shard_map/ppermute | solution.py:16
  412.3 6.3 %collective-permute-start.3 = (f32[4,18,1,130]{3,1,2,0:T(8,128)S(1)}, f32[4,18,1,130]{3,1,2,0:T(8,128)S(1)}, u32[]{:S(2)}, u32[]{:S(2)}) collective-permute-start(f32[4,18,1,130]{3,1,2,0:T(8,128)S(1)} %copy.163), channel_id=1, source_target_pairs={{1,0},{2,1},{3,2},{4,3},{5,4},{6,5},{7,6},{9,8},{10,9},{11,10},{12... | collective-permute-start | bytes 112328 | tf_op jit(solution)/shard_map/ppermute | solution.py:16
where the time goes:
time: 429 us; the launch traced here: 422 us
  matrix products  197 us (46%)
  local copies, waits for them, and re-layouts  111 us (26%)
  waiting for transfers between devices  59.5 us (14%)
  other arithmetic  35.5 us (8%)
  starting transfers between devices  15.9 us (4%)
    dot_general x16, matrix products, brick_tile(): lax.dot_general(columns, weight, (((1,), (1,)), ((), ())), precision=HIGH...  175 us
    all_to_all x1, waiting for transfers between devices, local(): lax.all_to_all(packed, ('gx', 'yz'), split_axis=0, concat_axis=0, tiled=T...  51.7 us
    slice x5, local copies, waits for them, and re-layouts, lay_last(): lower = arr[..., 0:8].reshape(lead + (8 * nbk,))  25.9 us
    mul x32, other arithmetic, brick_tile(): spread[0][:, None, None, :] * spread[1][None, :, None, :]  20 us
    dot_general x1, matrix products, local(): sums = jnp.einsum('sb,scn->bcn', pick, tiles, precision=HIGH)  18.9 us
    unnamed x18, local copies, waits for them, and re-layouts  15.6 us
    squeeze x16, local copies, waits for them, and re-layouts, local(): tiles = lax.map(jax.vmap(brick_tile), groups).reshape(slots, 13, 1000)  14.7 us
    concatenate x2, local copies, waits for them, and re-layouts, lay_last(): jnp.concatenate([arr[..., 8:10], jnp.zeros(lead + (nbk, 6), jnp.float32)]...  12.6 us
  transfers between devices with their start and end apart: 5, of which 5 were waited for; matrix products, arithmetic and copies ran while one was open for 0% of the time, Pallas kernels for 0%

commit v1 on v0

v1 whole, which is shorter than its diff:
```python
import functools

import jax
import jax.numpy as jnp
from jax import lax
from jax.experimental import pallas as pl
from jax.experimental.pallas import tpu as pltpu
from jax.sharding import PartitionSpec as P

SIDE = 16
DEPTH = 128
ROWS = 104
NCH = 17
NUV = 4


def pack_kernel(owners, bricks, cells, offsets, mass, velocity, affine, out, count):
    nblk = mass.shape[0]
    ndev = out.shape[0]
    out[:, NCH - 1] = jnp.full((ndev,) + out.shape[2:], -1.0, jnp.float32)

    def clear(i, carry):
        count[i] = 0
        return carry

    lax.fori_loop(0, ndev, clear, 0)

    def move(g, carry):
        d = owners[g]
        k = count[d]
        count[d] = k + 1
        slot = pl.ds(k, 1)
        for j in range(3):
            out[d, j, slot, :] = offsets[g, pl.ds(j, 1), :]
            out[d, 4 + j, slot, :] = velocity[g, pl.ds(j, 1), :]
        out[d, 3, slot, :] = mass[pl.ds(g, 1), :]
        for j in range(9):
            out[d, 7 + j, slot, :] = affine[g, pl.ds(j, 1), :]
        flat = cells[g, 0:1, :] * 64 + cells[g, 1:2, :] * 8 + cells[g, 2:3, :]
        out[d, 16, slot, :] = (flat + bricks[g] * 512).astype(jnp.float32)
        return carry

    lax.fori_loop(0, nblk, move, 0, unroll=2)


def halves(values):
    high = values.astype(jnp.bfloat16)
    low = (values - high.astype(jnp.float32)).astype(jnp.bfloat16)
    return high, low


def weights(place, frac):
    first = 0.5 * (1.5 - frac) ** 2
    middle = 0.75 - (frac - 1.0) ** 2
    last = 0.5 * (frac - 0.5) ** 2
    spread = jnp.where(place == 2.0, last, 0.0)
    spread = jnp.where(place == 1.0, middle, spread)
    return jnp.where(place == 0.0, first, spread)


def tile_kernel(codes, moved, grid, acc, chosen):
    ndev, _, cap, lanes = moved.shape
    slots = ndev * cap

    def choose(s, n):
        chosen[n] = s
        return n + jnp.where(codes[s] >= 0, 1, 0)

    total = lax.fori_loop(0, slots, choose, 0)
    acc[...] = jnp.zeros_like(acc)
    row = lax.broadcasted_iota(jnp.int32, (ROWS, lanes), 0)
    row_x = (row // 10).astype(jnp.float32)
    row_y = (row % 10).astype(jnp.float32)
    row_z = lax.broadcasted_iota(jnp.int32, (DEPTH, lanes), 0).astype(jnp.float32)

    def add_block(n, carry):
        s = chosen[n]
        d = s // cap
        slot = pl.ds(s % cap, 1)
        brick = codes[s] // 512
        uv = brick // (DEPTH // 8)
        w = brick % (DEPTH // 8)
        ch = lambda j: moved[d, j, slot, :]
        flat = ch(16).astype(jnp.int32) & 511
        cell_x = (flat // 64).astype(jnp.float32)
        cell_y = (flat // 8 % 8).astype(jnp.float32)
        cell_z = (flat % 8 + (w * 8 - 1)).astype(jnp.float32)
        fx, fy, fz = ch(0), ch(1), ch(2)
        m = ch(3)
        ex = row_x - cell_x
        ey = row_y - cell_y
        ez = row_z - cell_z
        rx = ex - fx
        ry = ey - fy
        rz = ez - fz
        wxy = weights(ex, fx) * weights(ey, fy)
        wz = weights(ez, fz)
        one = [wxy * m]
        two = [jnp.zeros((ROWS, lanes), jnp.float32)]
        for i in range(3):
            one.append(wxy * (m * ch(4 + i) + ch(7 + 3 * i) * rx + ch(8 + 3 * i) * ry))
            two.append(wxy * ch(9 + 3 * i))
        left = jnp.concatenate([jnp.concatenate(one, 0), jnp.concatenate(two, 0)], 1)
        right = jnp.concatenate([wz, wz * rz], 1)
        lh, ll = halves(left)
        rh, rl = halves(right)
        dims = (((1,), (1,)), ((), ()))
        both = lax.dot_general(
            lh, jnp.concatenate([rh, rl], 0), dims, preferred_element_type=jnp.float32
        )
        rest = lax.dot_general(ll, rh, dims, preferred_element_type=jnp.float32)
        acc[uv] += both[:, :DEPTH] + (both[:, DEPTH:] + rest)
        return carry

    lax.fori_loop(0, total, add_block, 0)
    grid[...] = jnp.zeros_like(grid)
    for uv in range(NUV):
        u, v = uv // 2, uv % 2
        for c in range(4):
            for x in range(10):
                base = c * ROWS + x * 10
                grid[c, 8 * u + x, 8 * v : 8 * v + 10, :] += acc[uv, base : base + 10, :]


def finish_kernel(grid, xlow, xhigh, ylow, yhigh, mass, speed):
    gx, yz = lax.axis_index("gx"), lax.axis_index("yz")
    last_x = SIDE * lax.axis_size("gx") - 1
    last_y = SIDE * lax.axis_size("yz") - 1
    shape = (SIDE, DEPTH)
    y = lax.broadcasted_iota(jnp.int32, shape, 0)
    ys = y + yz * SIDE
    z = lax.broadcasted_iota(jnp.int32, shape, 1)
    keep = (ys > 0) & (ys < last_y) & (z > 0) & (z < DEPTH - 1)
    for x in range(SIDE):
        inside = keep & (gx * SIDE + x > 0) & (gx * SIDE + x < last_x)
        scale = None
        for c in range(4):
            value = grid[c, x + 1, 1 : SIDE + 1, :]
            if x == 0:
                value = value + xlow[c, 1 : SIDE + 1, :]
            if x == SIDE - 1:
                value = value + xhigh[c, 1 : SIDE + 1, :]
            value = value + jnp.where(y == 0, ylow[c, x : x + 1, :], 0.0)
            value = value + jnp.where(y == SIDE - 1, yhigh[c, x : x + 1, :], 0.0)
            if c == 0:
                mass[x] = value
                scale = 1.0 / jnp.maximum(value, 0.5)
            else:
                value = value * scale
                if c == 3:
                    value = value - 0.5
                speed[c - 1, x] = jnp.where(inside, value, 0.0)


def passed_along(array, axis, by):
    devices = lax.axis_size(axis)
    pairs = [(i, i + by) for i in range(devices) if 0 <= i + by < devices]
    return lax.ppermute(array, axis, pairs)


VMEM = pl.BlockSpec(memory_space=pltpu.VMEM)
SMEM = pl.BlockSpec(memory_space=pltpu.SMEM)
PARAMS = pltpu.CompilerParams(vmem_limit_bytes=40 * 1024 * 1024)


def local(owners, bricks, cells, offsets, mass, velocity, affine):
    nblk, lanes = mass.shape
    ndev = lax.axis_size("gx") * lax.axis_size("yz")
    cap = 2 * nblk // ndev
    packed = pl.pallas_call(
        pack_kernel,
        out_shape=jax.ShapeDtypeStruct((ndev, NCH, cap, lanes), jnp.float32),
        in_specs=[SMEM, SMEM] + [VMEM] * 5,
        out_specs=VMEM,
        scratch_shapes=[pltpu.SMEM((ndev,), jnp.int32)],
        compiler_params=PARAMS,
        name="pack",
    )(owners[:, 0], bricks, cells, offsets, mass, velocity, affine)
    moved = lax.all_to_all(packed, ("gx", "yz"), split_axis=0, concat_axis=0, tiled=True)
    codes = moved[:, NCH - 1, :, 0].astype(jnp.int32).reshape(ndev * cap)
    grid = pl.pallas_call(
        tile_kernel,
        out_shape=jax.ShapeDtypeStruct((4, SIDE + 2, SIDE + 2, DEPTH), jnp.float32),
        in_specs=[SMEM, VMEM],
        out_specs=VMEM,
        scratch_shapes=[
            pltpu.VMEM((NUV, 4 * ROWS, DEPTH), jnp.float32),
            pltpu.SMEM((ndev * cap + 1,), jnp.int32),
        ],
        compiler_params=PARAMS,
        name="tiles",
    )(codes, moved)
    xlow = passed_along(grid[:, SIDE + 1], "gx", 1)
    xhigh = passed_along(grid[:, 0], "gx", -1)

    def y_face(at):
        face = grid[:, 1 : SIDE + 1, at]
        face = face.at[:, 0].add(xlow[:, at])
        return face.at[:, SIDE - 1].add(xhigh[:, at])

    ylow = passed_along(y_face(SIDE + 1), "yz", 1)
    yhigh = passed_along(y_face(0), "yz", -1)
    return pl.pallas_call(
        finish_kernel,
        out_shape=(
            jax.ShapeDtypeStruct((SIDE, SIDE, DEPTH), jnp.float32),
            jax.ShapeDtypeStruct((3, SIDE, SIDE, DEPTH), jnp.float32),
        ),
        in_specs=[VMEM] * 5,
        out_specs=(VMEM, VMEM),
        compiler_params=PARAMS,
        name="finish",
    )(grid, xlow, xhigh, ylow, yhigh)


def solution(mesh):
    block = ("gx", "yz")
    return jax.shard_map(
        local,
        mesh=mesh,
        in_specs=(
            P(block, None),
            P(block),
            P(block, None, None),
            P(block, None, None),
            P(block, None),
            P(block, None, None),
            P(block, None, None),
        ),
        out_specs=(P("gx", "yz", None), P(None, "gx", "yz", None)),
        check_vma=False,
    )
```

time: 429 us -> 173 us (0.40); the launches traced: 422 us -> 172 us
  matrix products: 197 us -> 0 us
  local copies, waits for them, and re-layouts: 111 us -> 4.97 us
  blocking collectives: 0 us -> 58.3 us
  Pallas kernels: 0 us -> 48.4 us
  other arithmetic: 35.5 us -> 0.63 us
  waiting for transfers between devices: 59.5 us -> 38.1 us
  starting transfers between devices: 15.9 us -> 20.7 us
    dot_general x18 -> x0, matrix products: 197 us -> none  [the longest x16 175 us: brick_tile(): lax.dot_general(columns, weight, (((1,), (1,)), ((), ())), precision=HIGH...]
    all_to_all x0 -> x1, blocking collectives: none -> 58.3 us  [local(): lax.all_to_all(packed, ('gx', 'yz'), split_axis=0, concat_axis=0, tiled=T...]
    all_to_all x1 -> x0, waiting for transfers between devices: 51.7 us -> none  [local(): lax.all_to_all(packed, ('gx', 'yz'), split_axis=0, concat_axis=0, tiled=T...]
    pallas_call x0 -> x3, Pallas kernels: none -> 48.4 us  [the longest x1 45.7 us: local(): pl.pallas_call(tile_kernel, out_shape=jax.ShapeDtypeStruct((4, SIDE + 2,...]
    ppermute x4, waiting for transfers between devices: 7.87 us -> 38.1 us  [passed_along(): return lax.ppermute(array, axis, pairs)]
    reshape x5 -> x0, local copies, waits for them, and re-layouts: 30 us -> none  [the longest x2 10.3 us: lay_last(): upper = jnp.concatenate([arr[..., 8:10], jnp.zeros(lead + (nbk, 6), jnp.f...]
    slice x47 -> x1, local copies, waits for them, and re-layouts: 29.6 us -> 0.05 us  [y_face(): face = grid[:, 1:SIDE + 1, at]]
    mul x33 -> x0, other arithmetic: 20.7 us -> none  [the longest x32 20 us: brick_tile(): spread[0][:, None, None, :] * spread[1][None, :, None, :]]
  transfers between devices with their start and end apart: 5 -> 4, of which waited for: 5 -> 2; matrix products, arithmetic and copies ran while one was open for 0% -> 0% of each run, Pallas kernels for 0% -> 0%
where the time goes in v1:
time: 173 us; the launch traced here: 172 us
  blocking collectives  58.3 us (34%)
  Pallas kernels  48.4 us (28%)
  waiting for transfers between devices  38.1 us (22%)
  starting transfers between devices  20.7 us (12%)
  local copies, waits for them, and re-layouts  4.97 us (3%)
    all_to_all x1, blocking collectives, local(): lax.all_to_all(packed, ('gx', 'yz'), split_axis=0, concat_axis=0, tiled=T...  58.3 us
    pallas_call x1, Pallas kernels, local(): pl.pallas_call(tile_kernel, out_shape=jax.ShapeDtypeStruct((4, SIDE + 2,...  45.7 us
    ppermute x4, waiting for transfers between devices, passed_along(): return lax.ppermute(array, axis, pairs)  38.1 us
    ppermute x4, starting transfers between devices, passed_along(): return lax.ppermute(array, axis, pairs)  20.7 us
    unnamed x10, local copies, waits for them, and re-layouts  4.68 us
  transfers between devices with their start and end apart: 4, of which 2 were waited for; matrix products, arithmetic and copies ran while one was open for 0% of the time, Pallas kernels for 0%

profile of v1, /device:TPU:5, one launch (start us, length us, event | category | flops | bytes accessed | tf_op | source)
XLA Modules:
  0.0 171.9 jit_solution(12276226948822839939)
XLA Ops:
  0.6 0.0 copy-start
  0.6 0.0 copy-start.2
  0.7 0.0 copy-start.1
  0.7 1.1 copy.19.cells
  1.8 1.1 copy.20.offsets
  2.8 1.1 copy.21.velocity
  3.9 1.4 copy.22.affine
  5.3 0.0 copy-done
  5.3 0.0 copy-done.2
  5.4 0.0 copy-done.1
  5.4 1.9 %pack.1 = f32[32,17,8,128]{3,2,1,0:T(8,128)S(1)} custom-call(s32[128]{0:T(128)S(1)} %bitcast.27, s32[128]{0:T(128)S(1)} %copy-done.2, s32[128,3,128]{2,1,0:T(4,128)S(1)} %copy.19.cells, f32[128,3,128]{2,1,0:T(4,128)S(1)} %copy.20.offsets, f32[128,128]{1,0:T(8,128)S(1)} %copy-done, f32[128,3,128]{2,1,0:T(4,128)S(1)} %copy.21.velocity, ...), custom_call_target="tpu_custom_call" | custom-call | tf_op jit(solution)/shard_map/pack/pallas_call | solution.py:170
  7.3 58.3 %all_to_all.5.moved = f32[32,17,8,128]{3,2,1,0:T(8,128)S(1)} all-to-all(f32[32,17,8,128]{3,2,1,0:T(8,128)S(1)} %pack.1), channel_id=1, replica_groups=mesh['gx'=4,'yz'=8] {'gx','yz'}, dimensions={0} | all-to-all | bytes 4456448 | tf_op jit(solution)/shard_map/all_to_all | solution.py:179
  65.5 0.6 fusion
  66.1 0.1 convert_element_type.8.codes
  66.2 45.7 %tiles.1.grid = f32[4,18,18,128]{3,2,1,0:T(8,128)S(1)} custom-call(s32[256]{0:T(256)S(1)} %convert_element_type.8.codes, f32[32,17,8,128]{3,2,1,0:T(8,128)S(1)} %all_to_all.5.moved), custom_call_target="tpu_custom_call" | custom-call | tf_op jit(solution)/shard_map/tiles/pallas_call | solution.py:181
  111.9 13.5 %collective-permute-start = (f32[4,18,128]{2,1,0:T(8,128)S(1)}, f32[4,18,128]{2,1,0:T(8,128)S(1)}, u32[]{:S(2)}, u32[]{:S(2)}) collective-permute-start(f32[4,18,128]{2,1,0:T(8,128)S(1)} %get-tuple-element.55), channel_id=1, source_target_pairs={{0,8},{8,16},{16,24},{1,9},{9,17},{17,25},{2,10},{10,18},{18,26},{... | collective-permute-start | bytes 110600 | tf_op jit(solution)/shard_map/ppermute | solution.py:158
  125.5 1.9 %collective-permute-start.1 = (f32[4,18,128]{2,1,0:T(8,128)S(1)}, f32[4,18,128]{2,1,0:T(8,128)S(1)}, u32[]{:S(2)}, u32[]{:S(2)}) collective-permute-start(f32[4,18,128]{2,1,0:T(8,128)S(1)} %get-tuple-element.54), channel_id=1, source_target_pairs={{8,0},{16,8},{24,16},{9,1},{17,9},{25,17},{10,2},{18,10},{26,18},{... | collective-permute-start | bytes 110600 | tf_op jit(solution)/shard_map/ppermute | solution.py:158
  127.5 0.0 collective-permute-done.xlow
  127.6 31.1 %collective-permute-done.1.xhigh = f32[4,18,128]{2,1,0:T(8,128)S(1)} collective-permute-done((f32[4,18,128]{2,1,0:T(8,128)S(1)}, f32[4,18,128]{2,1,0:T(8,128)S(1)}, u32[]{:S(2)}, u32[]{:S(2)}) %collective-permute-start.1) | collective-permute-done | bytes 36896 | tf_op jit(solution)/shard_map/ppermute | solution.py:158
  158.8 1.9 %collective-permute-start.2 = (f32[4,16,128]{2,1,0:T(8,128)S(1)}, f32[4,16,128]{2,1,0:T(8,128)S(1)}, u32[]{:S(2)}, u32[]{:S(2)}) collective-permute-start(f32[4,16,128]{2,1,0:T(8,128)S(1)} %scatter-add.15), channel_id=1, source_target_pairs={{0,1},{1,2},{2,3},{3,4},{4,5},{5,6},{6,7},{8,9},{9,10},{10,11},{11... | collective-permute-start | bytes 98312 | tf_op jit(solution)/shard_map/ppermute | solution.py:158
  160.7 3.4 %collective-permute-start.3 = (f32[4,16,128]{2,1,0:T(8,128)S(1)}, f32[4,16,128]{2,1,0:T(8,128)S(1)}, u32[]{:S(2)}, u32[]{:S(2)}) collective-permute-start(f32[4,16,128]{2,1,0:T(8,128)S(1)} %scatter-add.19), channel_id=1, source_target_pairs={{1,0},{2,1},{3,2},{4,3},{5,4},{6,5},{7,6},{9,8},{10,9},{11,10},{12... | collective-permute-start | bytes 98312 | tf_op jit(solution)/shard_map/ppermute | solution.py:158
  164.1 0.0 collective-permute-done.2.ylow
  164.1 6.9 %collective-permute-done.3.yhigh = f32[4,16,128]{2,1,0:T(8,128)S(1)} collective-permute-done((f32[4,16,128]{2,1,0:T(8,128)S(1)}, f32[4,16,128]{2,1,0:T(8,128)S(1)}, u32[]{:S(2)}, u32[]{:S(2)}) %collective-permute-start.3) | collective-permute-done | bytes 32800 | tf_op jit(solution)/shard_map/ppermute | solution.py:158
  171.0 0.9 finish.1
  (8 shorter events, 0.2 us)
Async XLA Ops:
  0.6 4.7 %copy-start = (f32[128,128]{1,0:T(8,128)S(1)}, f32[128,128]{1,0:T(8,128)}, u32[]{:S(2)}) copy-start(f32[128,128]{1,0:T(8,128)} %mass.1) | copy-start | bytes 196612
  0.6 4.7 %copy-start.2 = (s32[128]{0:T(128)S(1)}, s32[128]{0:T(128)}, u32[]{:S(2)}) copy-start(s32[128]{0:T(128)} %bricks.1) | copy-start | bytes 1540
  0.7 4.7 %copy-start.1 = (s32[128,1]{0,1:T(1,128)S(1)}, s32[128,1]{0,1:T(1,128)}, u32[]{:S(2)}) copy-start(s32[128,1]{0,1:T(1,128)} %param.15) | copy-start | bytes 1540
  111.9 15.5 %collective-permute-start = (f32[4,18,128]{2,1,0:T(8,128)S(1)}, f32[4,18,128]{2,1,0:T(8,128)S(1)}, u32[]{:S(2)}, u32[]{:S(2)}) collective-permute-start(f32[4,18,128]{2,1,0:T(8,128)S(1)} %get-tuple-element.55), channel_id=1, source_target_pairs={{0,8},{8,16},{16,24},{1,9},{9,17},{17,25},{2,10},{10,18},{18,26},{... | collective-permute-start | bytes 110600 | tf_op jit(solution)/shard_map/ppermute | solution.py:158
  125.5 33.1 %collective-permute-start.1 = (f32[4,18,128]{2,1,0:T(8,128)S(1)}, f32[4,18,128]{2,1,0:T(8,128)S(1)}, u32[]{:S(2)}, u32[]{:S(2)}) collective-permute-start(f32[4,18,128]{2,1,0:T(8,128)S(1)} %get-tuple-element.54), channel_id=1, source_target_pairs={{8,0},{16,8},{24,16},{9,1},{17,9},{25,17},{10,2},{18,10},{26,18},{... | collective-permute-start | bytes 110600 | tf_op jit(solution)/shard_map/ppermute | solution.py:158
  158.8 5.3 %collective-permute-start.2 = (f32[4,16,128]{2,1,0:T(8,128)S(1)}, f32[4,16,128]{2,1,0:T(8,128)S(1)}, u32[]{:S(2)}, u32[]{:S(2)}) collective-permute-start(f32[4,16,128]{2,1,0:T(8,128)S(1)} %scatter-add.15), channel_id=1, source_target_pairs={{0,1},{1,2},{2,3},{3,4},{4,5},{5,6},{6,7},{8,9},{9,10},{10,11},{11... | collective-permute-start | bytes 98312 | tf_op jit(solution)/shard_map/ppermute | solution.py:158
  160.7 10.3 %collective-permute-start.3 = (f32[4,16,128]{2,1,0:T(8,128)S(1)}, f32[4,16,128]{2,1,0:T(8,128)S(1)}, u32[]{:S(2)}, u32[]{:S(2)}) collective-permute-start(f32[4,16,128]{2,1,0:T(8,128)S(1)} %scatter-add.19), channel_id=1, source_target_pairs={{1,0},{2,1},{3,2},{4,3},{5,4},{6,5},{7,6},{9,8},{10,9},{11,10},{12... | collective-permute-start | bytes 98312 | tf_op jit(solution)/shard_map/ppermute | solution.py:158

commit v2 on v1

--- a/solution.py
+++ b/solution.py
@@ -12,35 +12,47 @@
 ROWS = 104
 NCH = 17
 NUV = 4
-
-
-def pack_kernel(owners, bricks, cells, offsets, mass, velocity, affine, out, count):
+PARTS = 2
+
+
+def pack_kernel(owners, bricks, cells, offsets, mass, velocity, affine, *rest):
+    outs, count = rest[:-1], rest[-1]
     nblk = mass.shape[0]
-    ndev = out.shape[0]
-    out[:, NCH - 1] = jnp.full((ndev,) + out.shape[2:], -1.0, jnp.float32)
+    ndev, _, part, lanes = outs[0].shape
+    for out in outs:
+        out[:, NCH - 1] = jnp.full((ndev, part, lanes), -1.0, jnp.float32)
 
     def clear(i, carry):
         count[i] = 0
         return carry
 
     lax.fori_loop(0, ndev, clear, 0)
+
+    def place(out, d, k, g):
+        slot = pl.ds(k, 1)
+        row = pl.ds(g, 1)
+        for j in range(3):
+            out[d, j, slot, :] = offsets[j, row, :]
+            out[d, 4 + j, slot, :] = velocity[j, row, :]
+        out[d, 3, slot, :] = mass[row, :]
+        for j in range(9):
+            out[d, 7 + j, slot, :] = affine[j, row, :]
+        flat = cells[0, row, :] * 64 + cells[1, row, :] * 8 + cells[2, row, :]
+        out[d, NCH - 1, slot, :] = (flat + bricks[g] * 512).astype(jnp.float32)
 
     def move(g, carry):
         d = owners[g]
         k = count[d]
         count[d] = k + 1
-        slot = pl.ds(k, 1)
-        for j in range(3):
-            out[d, j, slot, :] = offsets[g, pl.ds(j, 1), :]
-            out[d, 4 + j, slot, :] = velocity[g, pl.ds(j, 1), :]
-        out[d, 3, slot, :] = mass[pl.ds(g, 1), :]
-        for j in range(9):
-            out[d, 7 + j, slot, :] = affine[g, pl.ds(j, 1), :]
-        flat = cells[g, 0:1, :] * 64 + cells[g, 1:2, :] * 8 + cells[g, 2:3, :]
-        out[d, 16, slot, :] = (flat + bricks[g] * 512).astype(jnp.float32)
+        for i, out in enumerate(outs):
+
+            @pl.when((k >= i * part) & (k < (i + 1) * part))
+            def _(out=out, i=i):
+                place(out, d, k - i * part, g)
+
         return carry
 
-    lax.fori_loop(0, nblk, move, 0, unroll=2)
+    lax.fori_loop(0, nblk, move, 0)
 
 
 def halves(values):
@@ -58,68 +70,98 @@
     return jnp.where(place == 0.0, first, spread)
 
 
-def tile_kernel(codes, moved, grid, acc, chosen):
-    ndev, _, cap, lanes = moved.shape
-    slots = ndev * cap
+def tile_kernel(first, codes, moved, *rest):
+    acc, chosen = rest[-2:]
+    ndev, _, part, lanes = moved.shape
+    slots = ndev * part
 
     def choose(s, n):
         chosen[n] = s
         return n + jnp.where(codes[s] >= 0, 1, 0)
 
     total = lax.fori_loop(0, slots, choose, 0)
-    acc[...] = jnp.zeros_like(acc)
+    if first:
+        acc[...] = jnp.zeros_like(acc)
+    else:
+        acc[...] = rest[0][...]
     row = lax.broadcasted_iota(jnp.int32, (ROWS, lanes), 0)
     row_x = (row // 10).astype(jnp.float32)
-    row_y = (row % 10).astype(jnp.float32)
-    row_z = lax.broadcasted_iota(jnp.int32, (DEPTH, lanes), 0).astype(jnp.float32)
+    row_z = (row % 10).astype(jnp.float32)
+    row_y = lax.broadcasted_iota(jnp.int32, (16, lanes), 0).astype(jnp.float32)
+    none = jnp.zeros((16, lanes), jnp.float32)
+    fill = jnp.zeros((lanes - ROWS, 3 * lanes), jnp.float32)
 
     def add_block(n, carry):
         s = chosen[n]
-        d = s // cap
-        slot = pl.ds(s % cap, 1)
+        d = s // part
+        slot = pl.ds(s % part, 1)
         brick = codes[s] // 512
         uv = brick // (DEPTH // 8)
         w = brick % (DEPTH // 8)
         ch = lambda j: moved[d, j, slot, :]
-        flat = ch(16).astype(jnp.int32) & 511
-        cell_x = (flat // 64).astype(jnp.float32)
-        cell_y = (flat // 8 % 8).astype(jnp.float32)
-        cell_z = (flat % 8 + (w * 8 - 1)).astype(jnp.float32)
+        flat = ch(NCH - 1).astype(jnp.int32) & 511
+        cell_x = (flat >> 6).astype(jnp.float32)
+        cell_y = ((flat >> 3) & 7).astype(jnp.float32)
+        cell_z = (flat & 7).astype(jnp.float32)
         fx, fy, fz = ch(0), ch(1), ch(2)
         m = ch(3)
         ex = row_x - cell_x
         ey = row_y - cell_y
         ez = row_z - cell_z
-        rx = ex - fx
         ry = ey - fy
-        rz = ez - fz
-        wxy = weights(ex, fx) * weights(ey, fy)
-        wz = weights(ez, fz)
-        one = [wxy * m]
-        two = [jnp.zeros((ROWS, lanes), jnp.float32)]
+        wy = weights(ey, fy)
+        wxz = weights(ex, fx) * weights(ez, fz)
+        big = jnp.concatenate([wxz, wxz * (ex - fx), wxz * (ez - fz)], 1)
+        small = [jnp.concatenate([wy * m, none, none], 1)]
         for i in range(3):
-            one.append(wxy * (m * ch(4 + i) + ch(7 + 3 * i) * rx + ch(8 + 3 * i) * ry))
-            two.append(wxy * ch(9 + 3 * i))
-        left = jnp.concatenate([jnp.concatenate(one, 0), jnp.concatenate(two, 0)], 1)
-        right = jnp.concatenate([wz, wz * rz], 1)
-        lh, ll = halves(left)
-        rh, rl = halves(right)
-        dims = (((1,), (1,)), ((), ()))
+            plain = wy * (m * ch(4 + i) + ch(8 + 3 * i) * ry)
+            small.append(jnp.concatenate([plain, wy * ch(7 + 3 * i), wy * ch(9 + 3 * i)], 1))
+        sh, sl = halves(jnp.concatenate(small, 0))
+        bh, bl = halves(jnp.concatenate([big, fill], 0))
         both = lax.dot_general(
-            lh, jnp.concatenate([rh, rl], 0), dims, preferred_element_type=jnp.float32
+            jnp.concatenate([sh, sl], 0),
+            jnp.concatenate([bh, bl], 0),
+            (((1,), (1,)), ((), ())),
+            preferred_element_type=jnp.float32,
         )
-        rest = lax.dot_general(ll, rh, dims, preferred_element_type=jnp.float32)
-        acc[uv] += both[:, :DEPTH] + (both[:, DEPTH:] + rest)
+        acc[w, uv] += both[:64, :lanes] + (both[:64, lanes:] + both[64:, :lanes])
         return carry
 
     lax.fori_loop(0, total, add_block, 0)
+
+
+def place_kernel(acc, grid, wide, key):
+    depth_bricks = DEPTH // 8
+    rows = NUV * 64
+    for w in range(depth_bricks):
+        high, low = halves(acc[w].reshape(rows, DEPTH))
+        wide[:rows, w * DEPTH : (w + 1) * DEPTH] = high
+        wide[rows:, w * DEPTH : (w + 1) * DEPTH] = low
+    k = lax.broadcasted_iota(jnp.int32, key.shape, 0)
+    spot = k & (DEPTH - 1)
+    x = spot // 10
+    key[...] = x * 1024 + (spot - x * 10) + (k // DEPTH) * 8 - 1
+    lane = lax.broadcasted_iota(jnp.int32, key.shape, 1)
     grid[...] = jnp.zeros_like(grid)
-    for uv in range(NUV):
-        u, v = uv // 2, uv % 2
-        for c in range(4):
-            for x in range(10):
-                base = c * ROWS + x * 10
-                grid[c, 8 * u + x, 8 * v : 8 * v + 10, :] += acc[uv, base : base + 10, :]
+    for pair in range(5):
+        pick = jnp.concatenate(
+            [
+                jnp.where(key[...] == lane + (2 * pair + i) * 1024, 1.0, 0.0).astype(jnp.bfloat16)
+                for i in range(2)
+            ],
+            1,
+        )
+        put = jnp.dot(wide[...], pick, preferred_element_type=jnp.float32)
+        put = put[:rows] + put[rows:]
+        for i in range(2):
+            x = 2 * pair + i
+            for uv in range(NUV):
+                u, v = uv // 2, uv % 2
+                for c in range(4):
+                    base = uv * 64 + c * 16
+                    grid[c, 8 * u + x, 8 * v : 8 * v + 10, :] += put[
+                        base : base + 10, i * DEPTH : (i + 1) * DEPTH
+                    ]
 
 
 def finish_kernel(grid, xlow, xhigh, ylow, yhigh, mass, speed):
@@ -167,29 +209,57 @@
     nblk, lanes = mass.shape
     ndev = lax.axis_size("gx") * lax.axis_size("yz")
     cap = 2 * nblk // ndev
+    parts = PARTS
+    part = cap // parts
     packed = pl.pallas_call(
         pack_kernel,
-        out_shape=jax.ShapeDtypeStruct((ndev, NCH, cap, lanes), jnp.float32),
+        out_shape=[jax.ShapeDtypeStruct((ndev, NCH, part, lanes), jnp.float32)] * parts,
         in_specs=[SMEM, SMEM] + [VMEM] * 5,
-        out_specs=VMEM,
+        out_specs=[VMEM] * parts,
         scratch_shapes=[pltpu.SMEM((ndev,), jnp.int32)],
         compiler_params=PARAMS,
         name="pack",
-    )(owners[:, 0], bricks, cells, offsets, mass, velocity, affine)
-    moved = lax.all_to_all(packed, ("gx", "yz"), split_axis=0, concat_axis=0, tiled=True)
-    codes = moved[:, NCH - 1, :, 0].astype(jnp.int32).reshape(ndev * cap)
+    )(
+        owners[:, 0],
+        bricks,
+        jnp.transpose(cells, (1, 0, 2)),
+        jnp.transpose(offsets, (1, 0, 2)),
+        mass,
+        jnp.transpose(velocity, (1, 0, 2)),
+        jnp.transpose(affine, (1, 0, 2)),
+    )
+    moved = [
+        lax.all_to_all(p, ("gx", "yz"), split_axis=0, concat_axis=0, tiled=True) for p in packed
+    ]
+    sums = []
+    for arrived in moved:
+        codes = arrived[:, NCH - 1, :, 0].astype(jnp.int32).reshape(ndev * part)
+        sums = [
+            pl.pallas_call(
+                functools.partial(tile_kernel, not sums),
+                out_shape=jax.ShapeDtypeStruct((DEPTH // 8, NUV, 64, DEPTH), jnp.float32),
+                in_specs=[SMEM, VMEM] + [VMEM] * len(sums),
+                out_specs=VMEM,
+                scratch_shapes=[pltpu.SMEM((ndev * part + 1,), jnp.int32)],
+                compiler_params=PARAMS,
+                cost_estimate=pl.CostEstimate(
+                    flops=40_000_000_000 // parts, bytes_accessed=4_000_000, transcendentals=0
+                ),
+                name="tiles",
+            )(codes, arrived, *sums)
+        ]
     grid = pl.pallas_call(
-        tile_kernel,
+        place_kernel,
         out_shape=jax.ShapeDtypeStruct((4, SIDE + 2, SIDE + 2, DEPTH), jnp.float32),
-        in_specs=[SMEM, VMEM],
+        in_specs=[VMEM],
         out_specs=VMEM,
         scratch_shapes=[
-            pltpu.VMEM((NUV, 4 * ROWS, DEPTH), jnp.float32),
-            pltpu.SMEM((ndev * cap + 1,), jnp.int32),
+            pltpu.VMEM((2 * NUV * 64, (DEPTH // 8) * DEPTH), jnp.bfloat16),
+            pltpu.VMEM(((DEPTH // 8) * DEPTH, DEPTH), jnp.int32),
         ],
         compiler_params=PARAMS,
-        name="tiles",
-    )(codes, moved)
+        name="place",
+    )(*sums)
     xlow = passed_along(grid[:, SIDE + 1], "gx", 1)
     xhigh = passed_along(grid[:, 0], "gx", -1)
 

time: 173 us -> 166 us (0.960)
  blocking collectives: 58.3 us -> 34.4 us
  starting transfers between devices: 20.7 us -> 34.7 us
  waiting for transfers between devices: 38.1 us -> 33.8 us
  Pallas kernels: 48.4 us -> 52 us
    ppermute x4, waiting for transfers between devices: 38.1 us -> 6.52 us  [passed_along(): return lax.ppermute(array, axis, pairs)]
    all_to_all x0 -> x1, waiting for transfers between devices: none -> 27.3 us  [local(): lax.all_to_all(p, ('gx', 'yz'), split_axis=0, concat_axis=0, tiled=True)]
    all_to_all x1, blocking collectives: 58.3 us -> 34.4 us  [local(): lax.all_to_all(p, ('gx', 'yz'), split_axis=0, concat_axis=0, tiled=True)]
    ppermute x4, starting transfers between devices: 20.7 us -> 31.2 us  [passed_along(): return lax.ppermute(array, axis, pairs)]
    pallas_call x2 -> x4, Pallas kernels: 47.6 us -> 51.1 us  [the longest x2 41.5 us: local(): pl.pallas_call(functools.partial(tile_kernel, not sums), out_shape=jax.Sh...]
    all_to_all x0 -> x1, starting transfers between devices: none -> 3.52 us  [local(): lax.all_to_all(p, ('gx', 'yz'), split_axis=0, concat_axis=0, tiled=True)]
    unnamed x10 -> x14, local copies, waits for them, and re-layouts: 4.68 us -> 5.98 us
  transfers between devices with their start and end apart: 4 -> 5, of which waited for: 2 -> 3; matrix products, arithmetic and copies ran while one was open for 0% -> 1% of each run, Pallas kernels for 0% -> 0%
where the time goes in v2:
time: 166 us; the launch traced here: 163 us
  Pallas kernels  52 us (31%)
  starting transfers between devices  34.7 us (21%)
  blocking collectives  34.4 us (21%)
  waiting for transfers between devices  33.8 us (20%)
  local copies, waits for them, and re-layouts  6.4 us (4%)
    pallas_call x2, Pallas kernels, local(): pl.pallas_call(functools.partial(tile_kernel, not sums), out_shape=jax.Sh...  41.5 us
    all_to_all x1, blocking collectives, local(): lax.all_to_all(p, ('gx', 'yz'), split_axis=0, concat_axis=0, tiled=True)  34.4 us
    ppermute x4, starting transfers between devices, passed_along(): return lax.ppermute(array, axis, pairs)  31.2 us
    all_to_all x1, waiting for transfers between devices, local(): lax.all_to_all(p, ('gx', 'yz'), split_axis=0, concat_axis=0, tiled=True)  27.3 us
    ppermute x4, waiting for transfers between devices, passed_along(): return lax.ppermute(array, axis, pairs)  6.52 us
    pallas_call x1, Pallas kernels, local(): pl.pallas_call(pack_kernel, out_shape=[jax.ShapeDtypeStruct((ndev, NCH, p...  5.99 us
    unnamed x14, local copies, waits for them, and re-layouts  5.98 us
    pallas_call x1, Pallas kernels, local(): pl.pallas_call(place_kernel, out_shape=jax.ShapeDtypeStruct((4, SIDE + 2,...  3.6 us
  transfers between devices with their start and end apart: 5, of which 3 were waited for; matrix products, arithmetic and copies ran while one was open for 1% of the time, Pallas kernels for 0%

profile of v2, /device:TPU:5, one launch (start us, length us, event | category | flops | bytes accessed | tf_op | source)
XLA Modules:
  0.0 163.4 jit_solution(2129847986394063449)
XLA Ops:
  0.6 0.0 copy-start
  0.6 1.1 copy-done
  1.7 0.0 copy-start.1
  1.7 0.9 copy-done.1
  2.6 0.0 copy-start.2
  2.6 0.9 copy-done.2
  3.6 0.0 copy-start.3
  3.6 0.9 copy-done.3
  4.5 0.8 copy-done.4
  5.3 0.7 copy-done.5
  6.0 0.0 copy-start.6
  6.0 0.7 copy-done.6
  6.6 6.0 %pack.1 = (f32[32,17,4,128]{3,2,1,0:T(4,128)S(1)}, f32[32,17,4,128]{3,2,1,0:T(4,128)}) custom-call(s32[128]{0:T(128)S(1)} %bitcast.35, s32[128]{0:T(128)S(1)} %copy-done.6, s32[3,128,128]{2,1,0:T(8,128)S(1)} %bitcast.32, f32[3,128,128]{2,1,0:T(8,128)S(1)} %bitcast.33, f32[128,128]{1,0:T(8,128)S(1)} %copy-done.4, f32[3,128,128]{2,1,0:T(8,128)S(1)} %bitcast.34, ...), custom_call_target="tpu_custom_call" | custom-call | tf_op jit(solution)/shard_map/pack/pallas_call | solution.py:214
  12.6 34.4 %all_to_all.10.moved = f32[32,17,4,128]{3,2,1,0:T(4,128)S(1)} all-to-all(f32[32,17,4,128]{3,2,1,0:T(4,128)S(1)} %get-tuple-element.53), channel_id=1, replica_groups=mesh['gx'=4,'yz'=8] {'gx','yz'}, dimensions={0} | all-to-all | bytes 2228224 | tf_op jit(solution)/shard_map/all_to_all | solution.py:232
  47.0 3.5 %all-to-all-start = ((f32[32,17,4,128]{3,2,1,0:T(4,128)}), f32[32,17,4,128]{3,2,1,0:T(4,128)S(1)}, u32[]{:S(2)}, u32[]{:S(2)}) async-start(f32[32,17,4,128]{3,2,1,0:T(4,128)} %get-tuple-element.52), calls=%async_computation | async-start | bytes 2228224 | tf_op jit(solution)/shard_map/all_to_all | solution.py:232
  50.5 0.6 fusion
  51.2 0.1 convert_element_type.17.codes
  51.3 27.3 %all-to-all-done.moved = f32[32,17,4,128]{3,2,1,0:T(4,128)S(1)} async-done(((f32[32,17,4,128]{3,2,1,0:T(4,128)}), f32[32,17,4,128]{3,2,1,0:T(4,128)S(1)}, u32[]{:S(2)}, u32[]{:S(2)}) %all-to-all-start) | async-done | bytes 1114144 | tf_op jit(solution)/shard_map/all_to_all | solution.py:232
  78.6 0.6 fusion.1
  79.2 0.1 convert_element_type.15.codes
  79.3 32.7 %tiles.2.rest_0_ = f32[16,4,64,128]{3,2,1,0:T(8,128)S(1)} custom-call(s32[128]{0:T(128)S(1)} %convert_element_type.17.codes, f32[32,17,4,128]{3,2,1,0:T(4,128)S(1)} %all_to_all.10.moved), custom_call_target="tpu_custom_call" | custom-call | flops 20000000000 | bytes 4000000 | tf_op jit(solution)/shard_map/tiles/pallas_call | solution.py:238
  112.0 8.8 %tiles.3.acc = f32[16,4,64,128]{3,2,1,0:T(8,128)S(1)} custom-call(s32[128]{0:T(128)S(1)} %convert_element_type.15.codes, f32[32,17,4,128]{3,2,1,0:T(4,128)S(1)} %all-to-all-done.moved, f32[16,4,64,128]{3,2,1,0:T(8,128)S(1)} %tiles.2.rest_0_), custom_call_target="tpu_custom_call" | custom-call | flops 20000000000 | bytes 4000000 | tf_op jit(solution)/shard_map/tiles/pallas_call | solution.py:238
  120.8 3.6 %place.1.grid = f32[4,18,18,128]{3,2,1,0:T(8,128)S(1)} custom-call(f32[16,4,64,128]{3,2,1,0:T(8,128)S(1)} %tiles.3.acc), custom_call_target="tpu_custom_call" | custom-call | tf_op jit(solution)/shard_map/place/pallas_call | solution.py:251
  124.5 1.9 %collective-permute-start = (f32[4,18,128]{2,1,0:T(8,128)S(1)}, f32[4,18,128]{2,1,0:T(8,128)S(1)}, u32[]{:S(2)}, u32[]{:S(2)}) collective-permute-start(f32[4,18,128]{2,1,0:T(8,128)S(1)} %get-tuple-element.59), channel_id=1, source_target_pairs={{0,8},{8,16},{16,24},{1,9},{9,17},{17,25},{2,10},{10,18},{18,26},{... | collective-permute-start | bytes 110600 | tf_op jit(solution)/shard_map/ppermute | solution.py:200
  126.4 2.4 %collective-permute-start.1 = (f32[4,18,128]{2,1,0:T(8,128)S(1)}, f32[4,18,128]{2,1,0:T(8,128)S(1)}, u32[]{:S(2)}, u32[]{:S(2)}) collective-permute-start(f32[4,18,128]{2,1,0:T(8,128)S(1)} %get-tuple-element.58), channel_id=1, source_target_pairs={{8,0},{16,8},{24,16},{9,1},{17,9},{25,17},{10,2},{18,10},{26,18},{... | collective-permute-start | bytes 110600 | tf_op jit(solution)/shard_map/ppermute | solution.py:200
  128.9 0.0 collective-permute-done.xlow
  129.0 2.9 %collective-permute-done.1.xhigh = f32[4,18,128]{2,1,0:T(8,128)S(1)} collective-permute-done((f32[4,18,128]{2,1,0:T(8,128)S(1)}, f32[4,18,128]{2,1,0:T(8,128)S(1)}, u32[]{:S(2)}, u32[]{:S(2)}) %collective-permute-start.1) | collective-permute-done | bytes 36896 | tf_op jit(solution)/shard_map/ppermute | solution.py:200
  131.9 25.0 %collective-permute-start.2 = (f32[4,16,128]{2,1,0:T(8,128)S(1)}, f32[4,16,128]{2,1,0:T(8,128)S(1)}, u32[]{:S(2)}, u32[]{:S(2)}) collective-permute-start(f32[4,16,128]{2,1,0:T(8,128)S(1)} %scatter-add.15), channel_id=1, source_target_pairs={{0,1},{1,2},{2,3},{3,4},{4,5},{5,6},{6,7},{8,9},{9,10},{10,11},{11... | collective-permute-start | bytes 98312 | tf_op jit(solution)/shard_map/ppermute | solution.py:200
  156.9 1.9 %collective-permute-start.3 = (f32[4,16,128]{2,1,0:T(8,128)S(1)}, f32[4,16,128]{2,1,0:T(8,128)S(1)}, u32[]{:S(2)}, u32[]{:S(2)}) collective-permute-start(f32[4,16,128]{2,1,0:T(8,128)S(1)} %scatter-add.19), channel_id=1, source_target_pairs={{1,0},{2,1},{3,2},{4,3},{5,4},{6,5},{7,6},{9,8},{10,9},{11,10},{12... | collective-permute-start | bytes 98312 | tf_op jit(solution)/shard_map/ppermute | solution.py:200
  158.9 0.0 collective-permute-done.2.ylow
  158.9 3.6 %collective-permute-done.3.yhigh = f32[4,16,128]{2,1,0:T(8,128)S(1)} collective-permute-done((f32[4,16,128]{2,1,0:T(8,128)S(1)}, f32[4,16,128]{2,1,0:T(8,128)S(1)}, u32[]{:S(2)}, u32[]{:S(2)}) %collective-permute-start.3) | collective-permute-done | bytes 32800 | tf_op jit(solution)/shard_map/ppermute | solution.py:200
  162.5 0.9 finish.1
  (10 shorter events, 0.2 us)
Async XLA Ops:
  0.6 1.1 copy-start
  1.7 0.9 copy-start.1
  2.6 0.9 copy-start.2
  3.6 0.9 copy-start.3
  4.5 0.8 copy-start.4
  5.3 0.7 copy-start.5
  6.0 0.7 copy-start.6
  47.0 31.5 %all-to-all-start = ((f32[32,17,4,128]{3,2,1,0:T(4,128)}), f32[32,17,4,128]{3,2,1,0:T(4,128)S(1)}, u32[]{:S(2)}, u32[]{:S(2)}) async-start(f32[32,17,4,128]{3,2,1,0:T(4,128)} %get-tuple-element.52), calls=%async_computation | async-start | bytes 2228224 | tf_op jit(solution)/shard_map/all_to_all | solution.py:232
  124.5 4.4 %collective-permute-start = (f32[4,18,128]{2,1,0:T(8,128)S(1)}, f32[4,18,128]{2,1,0:T(8,128)S(1)}, u32[]{:S(2)}, u32[]{:S(2)}) collective-permute-start(f32[4,18,128]{2,1,0:T(8,128)S(1)} %get-tuple-element.59), channel_id=1, source_target_pairs={{0,8},{8,16},{16,24},{1,9},{9,17},{17,25},{2,10},{10,18},{18,26},{... | collective-permute-start | bytes 110600 | tf_op jit(solution)/shard_map/ppermute | solution.py:200
  126.4 5.4 %collective-permute-start.1 = (f32[4,18,128]{2,1,0:T(8,128)S(1)}, f32[4,18,128]{2,1,0:T(8,128)S(1)}, u32[]{:S(2)}, u32[]{:S(2)}) collective-permute-start(f32[4,18,128]{2,1,0:T(8,128)S(1)} %get-tuple-element.58), channel_id=1, source_target_pairs={{8,0},{16,8},{24,16},{9,1},{17,9},{25,17},{10,2},{18,10},{26,18},{... | collective-permute-start | bytes 110600 | tf_op jit(solution)/shard_map/ppermute | solution.py:200
  131.9 26.9 %collective-permute-start.2 = (f32[4,16,128]{2,1,0:T(8,128)S(1)}, f32[4,16,128]{2,1,0:T(8,128)S(1)}, u32[]{:S(2)}, u32[]{:S(2)}) collective-permute-start(f32[4,16,128]{2,1,0:T(8,128)S(1)} %scatter-add.15), channel_id=1, source_target_pairs={{0,1},{1,2},{2,3},{3,4},{4,5},{5,6},{6,7},{8,9},{9,10},{10,11},{11... | collective-permute-start | bytes 98312 | tf_op jit(solution)/shard_map/ppermute | solution.py:200
  156.9 5.6 %collective-permute-start.3 = (f32[4,16,128]{2,1,0:T(8,128)S(1)}, f32[4,16,128]{2,1,0:T(8,128)S(1)}, u32[]{:S(2)}, u32[]{:S(2)}) collective-permute-start(f32[4,16,128]{2,1,0:T(8,128)S(1)} %scatter-add.19), channel_id=1, source_target_pairs={{1,0},{2,1},{3,2},{4,3},{5,4},{6,5},{7,6},{9,8},{10,9},{11,10},{12... | collective-permute-start | bytes 98312 | tf_op jit(solution)/shard_map/ppermute | solution.py:200

commit v3 on v2

--- a/solution.py
+++ b/solution.py
@@ -12,11 +12,17 @@
 ROWS = 104
 NCH = 17
 NUV = 4
-PARTS = 2
-
-
-def pack_kernel(owners, bricks, cells, offsets, mass, velocity, affine, *rest):
-    outs, count = rest[:-1], rest[-1]
+PARTS = 4
+GROUP = 2
+
+
+def pack_kernel(owners, bricks, *rest, parts):
+    sources, outs = rest[:5], rest[5 : 5 + parts]
+    held, (count, listed, slots, sems) = rest[5 + parts : 10 + parts], rest[10 + parts :]
+    copies = [pltpu.make_async_copy(s, h, sems.at[i]) for i, (s, h) in enumerate(zip(sources, held))]
+    for copy in copies:
+        copy.start()
+    cells, offsets, mass, velocity, affine = held
     nblk = mass.shape[0]
     ndev, _, part, lanes = outs[0].shape
     for out in outs:
@@ -28,31 +34,40 @@
 
     lax.fori_loop(0, ndev, clear, 0)
 
-    def place(out, d, k, g):
-        slot = pl.ds(k, 1)
-        row = pl.ds(g, 1)
-        for j in range(3):
-            out[d, j, slot, :] = offsets[j, row, :]
-            out[d, 4 + j, slot, :] = velocity[j, row, :]
-        out[d, 3, slot, :] = mass[row, :]
-        for j in range(9):
-            out[d, 7 + j, slot, :] = affine[j, row, :]
-        flat = cells[0, row, :] * 64 + cells[1, row, :] * 8 + cells[2, row, :]
-        out[d, NCH - 1, slot, :] = (flat + bricks[g] * 512).astype(jnp.float32)
-
-    def move(g, carry):
+    def rank(g, sizes):
         d = owners[g]
         k = count[d]
         count[d] = k + 1
-        for i, out in enumerate(outs):
-
-            @pl.when((k >= i * part) & (k < (i + 1) * part))
-            def _(out=out, i=i):
-                place(out, d, k - i * part, g)
-
-        return carry
-
-    lax.fori_loop(0, nblk, move, 0)
+        mine = k // part
+        grown = []
+        for i in range(parts):
+            listed[i * (nblk + 1) + sizes[i]] = g
+            slots[i * (nblk + 1) + sizes[i]] = d * part + k % part
+            grown.append(sizes[i] + jnp.where(mine == i, 1, 0))
+        return tuple(grown)
+
+    sizes = lax.fori_loop(0, nblk, rank, (0,) * parts)
+    for copy in copies:
+        copy.wait()
+    for i, out in enumerate(outs):
+
+        def move(n, carry, i=i, out=out):
+            g = listed[i * (nblk + 1) + n]
+            at = slots[i * (nblk + 1) + n]
+            d = at // part
+            slot = pl.ds(at % part, 1)
+            row = pl.ds(g, 1)
+            for j in range(3):
+                out[d, j, slot, :] = offsets[j, row, :]
+                out[d, 4 + j, slot, :] = velocity[j, row, :]
+            out[d, 3, slot, :] = mass[row, :]
+            for j in range(9):
+                out[d, 7 + j, slot, :] = affine[j, row, :]
+            flat = cells[0, row, :] * 64 + cells[1, row, :] * 8 + cells[2, row, :]
+            out[d, NCH - 1, slot, :] = (flat + bricks[g] * 512).astype(jnp.float32)
+            return carry
+
+        lax.fori_loop(0, sizes[i], move, 0)
 
 
 def halves(values):
@@ -91,7 +106,7 @@
     none = jnp.zeros((16, lanes), jnp.float32)
     fill = jnp.zeros((lanes - ROWS, 3 * lanes), jnp.float32)
 
-    def add_block(n, carry):
+    def block(n):
         s = chosen[n]
         d = s // part
         slot = pl.ds(s % part, 1)
@@ -124,10 +139,16 @@
             (((1,), (1,)), ((), ())),
             preferred_element_type=jnp.float32,
         )
-        acc[w, uv] += both[:64, :lanes] + (both[:64, lanes:] + both[64:, :lanes])
+        return w, uv, both[:64, :lanes] + (both[:64, lanes:] + both[64:, :lanes])
+
+    def add_blocks(n, carry, group):
+        for w, uv, tile in [block(n + i) for i in range(group)]:
+            acc[w, uv] += tile
         return carry
 
-    lax.fori_loop(0, total, add_block, 0)
+    paired = total // GROUP * GROUP
+    lax.fori_loop(0, total // GROUP, lambda n, c: add_blocks(n * GROUP, c, GROUP), 0)
+    lax.fori_loop(paired, total, lambda n, c: add_blocks(n, c, 1), 0)
 
 
 def place_kernel(acc, grid, wide, key):
@@ -201,6 +222,7 @@
 
 
 VMEM = pl.BlockSpec(memory_space=pltpu.VMEM)
+HBM = pl.BlockSpec(memory_space=pltpu.HBM)
 SMEM = pl.BlockSpec(memory_space=pltpu.SMEM)
 PARAMS = pltpu.CompilerParams(vmem_limit_bytes=40 * 1024 * 1024)
 
@@ -209,15 +231,24 @@
     nblk, lanes = mass.shape
     ndev = lax.axis_size("gx") * lax.axis_size("yz")
     cap = 2 * nblk // ndev
-    parts = PARTS
+    parts = min(PARTS, cap)
     part = cap // parts
     packed = pl.pallas_call(
-        pack_kernel,
+        functools.partial(pack_kernel, parts=parts),
         out_shape=[jax.ShapeDtypeStruct((ndev, NCH, part, lanes), jnp.float32)] * parts,
-        in_specs=[SMEM, SMEM] + [VMEM] * 5,
+        in_specs=[SMEM, SMEM] + [HBM] * 5,
         out_specs=[VMEM] * parts,
-        scratch_shapes=[pltpu.SMEM((ndev,), jnp.int32)],
-        compiler_params=PARAMS,
+        scratch_shapes=[
+            pltpu.VMEM((3, nblk, lanes), jnp.int32),
+            pltpu.VMEM((3, nblk, lanes), jnp.float32),
+            pltpu.VMEM((nblk, lanes), jnp.float32),
+            pltpu.VMEM((3, nblk, lanes), jnp.float32),
+            pltpu.VMEM((9, nblk, lanes), jnp.float32),
+            pltpu.SMEM((ndev,), jnp.int32),
+            pltpu.SMEM((parts * (nblk + 1),), jnp.int32),
+            pltpu.SMEM((parts * (nblk + 1),), jnp.int32),
+            pltpu.SemaphoreType.DMA((5,)),
+        ],
         name="pack",
     )(
         owners[:, 0],
@@ -228,9 +259,11 @@
         jnp.transpose(velocity, (1, 0, 2)),
         jnp.transpose(affine, (1, 0, 2)),
     )
-    moved = [
-        lax.all_to_all(p, ("gx", "yz"), split_axis=0, concat_axis=0, tiled=True) for p in packed
-    ]
+    moved = []
+    for p in packed:
+        if moved:
+            p, moved[-1] = lax.optimization_barrier((p, moved[-1]))
+        moved.append(lax.all_to_all(p, ("gx", "yz"), split_axis=0, concat_axis=0, tiled=True))
     sums = []
     for arrived in moved:
         codes = arrived[:, NCH - 1, :, 0].astype(jnp.int32).reshape(ndev * part)

time: 166 us -> 140 us (0.84)
  the two profiles are of different devices: /device:TPU:5 before, /device:TPU:17 now
where the time goes in v3:
time: 140 us; the launch traced here: 139 us
  starting transfers between devices  50.4 us (36%)
  blocking collectives  39.4 us (28%)
  Pallas kernels  28.8 us (21%)
  local copies, waits for them, and re-layouts  9.42 us (7%)
  waiting for transfers between devices  7.94 us (6%)
  other arithmetic  2.47 us (2%)
    all_to_all x2, blocking collectives, local(): lax.all_to_all(p, ('gx', 'yz'), split_axis=0, concat_axis=0, tiled=True)  39.4 us
    ppermute x4, starting transfers between devices, passed_along(): return lax.ppermute(array, axis, pairs)  38.4 us
    pallas_call x4, Pallas kernels, local(): pl.pallas_call(functools.partial(tile_kernel, not sums), out_shape=jax.Sh...  16.2 us
    all_to_all x2, starting transfers between devices, local(): lax.all_to_all(p, ('gx', 'yz'), split_axis=0, concat_axis=0, tiled=True)  12 us
    unnamed x12, local copies, waits for them, and re-layouts  8.78 us
    pallas_call x1, Pallas kernels, local(): pl.pallas_call(functools.partial(pack_kernel, parts=parts), out_shape=[ja...  8.13 us
    ppermute x4, waiting for transfers between devices, passed_along(): return lax.ppermute(array, axis, pairs)  4.38 us
    pallas_call x1, Pallas kernels, local(): pl.pallas_call(place_kernel, out_shape=jax.ShapeDtypeStruct((4, SIDE + 2,...  3.6 us
  transfers between devices with their start and end apart: 6, of which 3 were waited for; matrix products, arithmetic and copies ran while one was open for 2% of the time, Pallas kernels for 11%

profile of v3, /device:TPU:17, one launch (start us, length us, event | category | flops | bytes accessed | tf_op | source)
XLA Modules:
  0.0 139.3 jit_solution(15767014385364483730)
XLA Ops:
  0.6 8.1 %pack.1 = (f32[32,17,2,128]{3,2,1,0:T(2,128)}, f32[32,17,2,128]{3,2,1,0:T(2,128)}, f32[32,17,2,128]{3,2,1,0:T(2,128)}, f32[32,17,2,128]{3,2,1,0:T(2,128)}) custom-call(s32[128]{0:T(128)} %bitcast.37, s32[128]{0:T(128)} %bricks.1, s32[3,128,128]{2,1,0:T(8,128)} %bitcast.32, f32[3,128,128]{2,1,0:T(8,128)} %bitcast.33, f32[128,128]{1,0:T(8,128)} %rest_2_.1, ...), custom_call_target="tpu_custom_call" | custom-call | tf_op jit(solution)/shard_map/pack/pallas_call | solution.py:236
  8.8 19.9 %all_to_all.20.moved = f32[32,17,2,128]{3,2,1,0:T(2,128)S(1)} all-to-all(f32[32,17,2,128]{3,2,1,0:T(2,128)} %get-tuple-element.63), channel_id=1, replica_groups=mesh['gx'=4,'yz'=8] {'gx','yz'}, dimensions={0} | all-to-all | bytes 1114112 | tf_op jit(solution)/shard_map/all_to_all | solution.py:266
  28.6 19.5 %all_to_all.21.moved = f32[32,17,2,128]{3,2,1,0:T(2,128)S(1)} all-to-all(f32[32,17,2,128]{3,2,1,0:T(2,128)} %get-tuple-element.64), channel_id=1, replica_groups=mesh['gx'=4,'yz'=8] {'gx','yz'}, dimensions={0} | all-to-all | bytes 1114112 | tf_op jit(solution)/shard_map/all_to_all | solution.py:266
  48.2 6.2 %all-to-all-start.2 = ((f32[32,17,2,128]{3,2,1,0:T(2,128)}), f32[32,17,2,128]{3,2,1,0:T(2,128)S(1)}, u32[]{:S(2)}, u32[]{:S(2)}) async-start(f32[32,17,2,128]{3,2,1,0:T(2,128)} %get-tuple-element.65), calls=%async_computation.2 | async-start | bytes 1114112 | tf_op jit(solution)/shard_map/all_to_all | solution.py:266
  54.3 0.6 convert_reduce_fusion
  55.0 0.1 convert_element_type.35.codes
  55.1 11.7 %tiles.4.rest_0_ = f32[16,4,64,128]{3,2,1,0:T(8,128)S(1)} custom-call(s32[64]{0:T(128)S(1)} %convert_element_type.35.codes, f32[32,17,2,128]{3,2,1,0:T(2,128)S(1)} %all_to_all.20.moved), custom_call_target="tpu_custom_call" | custom-call | flops 10000000000 | bytes 4000000 | tf_op jit(solution)/shard_map/tiles/pallas_call | solution.py:271
  66.8 1.3 copy-done
  68.1 0.6 convert_reduce_fusion.1
  68.7 0.1 convert_element_type.33.codes
  68.8 5.9 %all-to-all-start.3 = ((f32[32,17,2,128]{3,2,1,0:T(2,128)}), f32[32,17,2,128]{3,2,1,0:T(2,128)S(1)}, u32[]{:S(2)}, u32[]{:S(2)}) async-start(f32[32,17,2,128]{3,2,1,0:T(2,128)} %get-tuple-element.66), calls=%async_computation.3 | async-start | bytes 1114112 | tf_op jit(solution)/shard_map/all_to_all | solution.py:266
  74.7 1.6 %copy-done.1 = f32[16,4,64,128]{3,2,1,0:T(8,128)S(1)} copy-done((f32[16,4,64,128]{3,2,1,0:T(8,128)S(1)}, f32[16,4,64,128]{3,2,1,0:T(8,128)}, u32[]{:S(2)}) %copy-start.1) | copy-done | bytes 2097176
  76.3 2.0 %tiles.5.rest_0_ = f32[16,4,64,128]{3,2,1,0:T(8,128)S(1)} custom-call(s32[64]{0:T(128)S(1)} %convert_element_type.33.codes, f32[32,17,2,128]{3,2,1,0:T(2,128)S(1)} %all_to_all.21.moved, f32[16,4,64,128]{3,2,1,0:T(8,128)S(1)} %copy-done.1), custom_call_target="tpu_custom_call" | custom-call | flops 10000000000 | bytes 4000000 | tf_op jit(solution)/shard_map/tiles/pallas_call | solution.py:271
  78.3 1.3 copy-done.4
  79.7 0.6 convert_reduce_fusion.2
  80.3 0.1 convert_element_type.31.codes
  80.4 1.6 %copy-done.5 = f32[16,4,64,128]{3,2,1,0:T(8,128)S(1)} copy-done((f32[16,4,64,128]{3,2,1,0:T(8,128)S(1)}, f32[16,4,64,128]{3,2,1,0:T(8,128)}, u32[]{:S(2)}) %copy-start.5) | copy-done | bytes 2097176
  82.0 1.4 tiles.6.rest_0_
  83.4 1.3 copy-done.2
  84.7 3.6 %all-to-all-done.3.moved = f32[32,17,2,128]{3,2,1,0:T(2,128)S(1)} async-done(((f32[32,17,2,128]{3,2,1,0:T(2,128)}), f32[32,17,2,128]{3,2,1,0:T(2,128)S(1)}, u32[]{:S(2)}, u32[]{:S(2)}) %all-to-all-start.3) | async-done | bytes 557088 | tf_op jit(solution)/shard_map/all_to_all | solution.py:266
  88.3 0.6 fusion
  88.9 0.1 convert_element_type.29.codes
  89.0 1.6 %copy-done.3 = f32[16,4,64,128]{3,2,1,0:T(8,128)S(1)} copy-done((f32[16,4,64,128]{3,2,1,0:T(8,128)S(1)}, f32[16,4,64,128]{3,2,1,0:T(8,128)}, u32[]{:S(2)}) %copy-start.3) | copy-done | bytes 2097176
  90.6 1.1 tiles.7.acc
  91.8 3.6 %place.1.grid = f32[4,18,18,128]{3,2,1,0:T(8,128)S(1)} custom-call(f32[16,4,64,128]{3,2,1,0:T(8,128)S(1)} %tiles.7.acc), custom_call_target="tpu_custom_call" | custom-call | tf_op jit(solution)/shard_map/place/pallas_call | solution.py:284
  95.4 2.4 %collective-permute-start = (f32[4,18,128]{2,1,0:T(8,128)S(1)}, f32[4,18,128]{2,1,0:T(8,128)S(1)}, u32[]{:S(2)}, u32[]{:S(2)}) collective-permute-start(f32[4,18,128]{2,1,0:T(8,128)S(1)} %get-tuple-element.75), channel_id=1, source_target_pairs={{0,8},{8,16},{16,24},{1,9},{9,17},{17,25},{2,10},{10,18},{18,26},{... | collective-permute-start | bytes 110600 | tf_op jit(solution)/shard_map/ppermute | solution.py:221
  97.8 26.2 %collective-permute-start.1 = (f32[4,18,128]{2,1,0:T(8,128)S(1)}, f32[4,18,128]{2,1,0:T(8,128)S(1)}, u32[]{:S(2)}, u32[]{:S(2)}) collective-permute-start(f32[4,18,128]{2,1,0:T(8,128)S(1)} %get-tuple-element.74), channel_id=1, source_target_pairs={{8,0},{16,8},{24,16},{9,1},{17,9},{25,17},{10,2},{18,10},{26,18},{... | collective-permute-start | bytes 110600 | tf_op jit(solution)/shard_map/ppermute | solution.py:221
  124.2 0.8 collective-permute-done.1.xhigh
  125.0 7.8 %collective-permute-start.3 = (f32[4,16,128]{2,1,0:T(8,128)S(1)}, f32[4,16,128]{2,1,0:T(8,128)S(1)}, u32[]{:S(2)}, u32[]{:S(2)}) collective-permute-start(f32[4,16,128]{2,1,0:T(8,128)S(1)} %scatter-add.19), channel_id=1, source_target_pairs={{1,0},{2,1},{3,2},{4,3},{5,4},{6,5},{7,6},{9,8},{10,9},{11,10},{12... | collective-permute-start | bytes 98312 | tf_op jit(solution)/shard_map/ppermute | solution.py:221
  132.9 1.9 %collective-permute-start.2 = (f32[4,16,128]{2,1,0:T(8,128)S(1)}, f32[4,16,128]{2,1,0:T(8,128)S(1)}, u32[]{:S(2)}, u32[]{:S(2)}) collective-permute-start(f32[4,16,128]{2,1,0:T(8,128)S(1)} %scatter-add.15), channel_id=1, source_target_pairs={{0,1},{1,2},{2,3},{3,4},{4,5},{5,6},{6,7},{8,9},{9,10},{10,11},{11... | collective-permute-start | bytes 98312 | tf_op jit(solution)/shard_map/ppermute | solution.py:221
  134.8 3.6 %collective-permute-done.2.ylow = f32[4,16,128]{2,1,0:T(8,128)S(1)} collective-permute-done((f32[4,16,128]{2,1,0:T(8,128)S(1)}, f32[4,16,128]{2,1,0:T(8,128)S(1)}, u32[]{:S(2)}, u32[]{:S(2)}) %collective-permute-start.2) | collective-permute-done | bytes 32800 | tf_op jit(solution)/shard_map/ppermute | solution.py:221
  138.4 0.9 finish.1
  (17 shorter events, 0.2 us)
Async XLA Ops:
  48.2 20.7 %all-to-all-start.2 = ((f32[32,17,2,128]{3,2,1,0:T(2,128)}), f32[32,17,2,128]{3,2,1,0:T(2,128)S(1)}, u32[]{:S(2)}, u32[]{:S(2)}) async-start(f32[32,17,2,128]{3,2,1,0:T(2,128)} %get-tuple-element.65), calls=%async_computation.2 | async-start | bytes 1114112 | tf_op jit(solution)/shard_map/all_to_all | solution.py:266
  66.7 1.3 copy-start
  68.8 19.5 %all-to-all-start.3 = ((f32[32,17,2,128]{3,2,1,0:T(2,128)}), f32[32,17,2,128]{3,2,1,0:T(2,128)S(1)}, u32[]{:S(2)}, u32[]{:S(2)}) async-start(f32[32,17,2,128]{3,2,1,0:T(2,128)} %get-tuple-element.66), calls=%async_computation.3 | async-start | bytes 1114112 | tf_op jit(solution)/shard_map/all_to_all | solution.py:266
  74.7 1.6 %copy-start.1 = (f32[16,4,64,128]{3,2,1,0:T(8,128)S(1)}, f32[16,4,64,128]{3,2,1,0:T(8,128)}, u32[]{:S(2)}) copy-start(f32[16,4,64,128]{3,2,1,0:T(8,128)} %copy-done) | copy-start | bytes 6291460
  78.3 1.3 copy-start.4
  80.4 1.6 %copy-start.5 = (f32[16,4,64,128]{3,2,1,0:T(8,128)S(1)}, f32[16,4,64,128]{3,2,1,0:T(8,128)}, u32[]{:S(2)}) copy-start(f32[16,4,64,128]{3,2,1,0:T(8,128)} %copy-done.4) | copy-start | bytes 6291460
  83.4 1.3 copy-start.2
  89.0 1.6 %copy-start.3 = (f32[16,4,64,128]{3,2,1,0:T(8,128)S(1)}, f32[16,4,64,128]{3,2,1,0:T(8,128)}, u32[]{:S(2)}) copy-start(f32[16,4,64,128]{3,2,1,0:T(8,128)} %copy-done.2) | copy-start | bytes 6291460
  95.4 28.7 %collective-permute-start = (f32[4,18,128]{2,1,0:T(8,128)S(1)}, f32[4,18,128]{2,1,0:T(8,128)S(1)}, u32[]{:S(2)}, u32[]{:S(2)}) collective-permute-start(f32[4,18,128]{2,1,0:T(8,128)S(1)} %get-tuple-element.75), channel_id=1, source_target_pairs={{0,8},{8,16},{16,24},{1,9},{9,17},{17,25},{2,10},{10,18},{18,26},{... | collective-permute-start | bytes 110600 | tf_op jit(solution)/shard_map/ppermute | solution.py:221
  97.8 27.1 %collective-permute-start.1 = (f32[4,18,128]{2,1,0:T(8,128)S(1)}, f32[4,18,128]{2,1,0:T(8,128)S(1)}, u32[]{:S(2)}, u32[]{:S(2)}) collective-permute-start(f32[4,18,128]{2,1,0:T(8,128)S(1)} %get-tuple-element.74), channel_id=1, source_target_pairs={{8,0},{16,8},{24,16},{9,1},{17,9},{25,17},{10,2},{18,10},{26,18},{... | collective-permute-start | bytes 110600 | tf_op jit(solution)/shard_map/ppermute | solution.py:221
  125.0 9.8 %collective-permute-start.3 = (f32[4,16,128]{2,1,0:T(8,128)S(1)}, f32[4,16,128]{2,1,0:T(8,128)S(1)}, u32[]{:S(2)}, u32[]{:S(2)}) collective-permute-start(f32[4,16,128]{2,1,0:T(8,128)S(1)} %scatter-add.19), channel_id=1, source_target_pairs={{1,0},{2,1},{3,2},{4,3},{5,4},{6,5},{7,6},{9,8},{10,9},{11,10},{12... | collective-permute-start | bytes 98312 | tf_op jit(solution)/shard_map/ppermute | solution.py:221
  132.9 5.6 %collective-permute-start.2 = (f32[4,16,128]{2,1,0:T(8,128)S(1)}, f32[4,16,128]{2,1,0:T(8,128)S(1)}, u32[]{:S(2)}, u32[]{:S(2)}) collective-permute-start(f32[4,16,128]{2,1,0:T(8,128)S(1)} %scatter-add.15), channel_id=1, source_target_pairs={{0,1},{1,2},{2,3},{3,4},{4,5},{5,6},{6,7},{8,9},{9,10},{10,11},{11... | collective-permute-start | bytes 98312 | tf_op jit(solution)/shard_map/ppermute | solution.py:221

commit v4 on v3

--- a/solution.py
+++ b/solution.py
@@ -12,8 +12,8 @@
 ROWS = 104
 NCH = 17
 NUV = 4
-PARTS = 4
-GROUP = 2
+PARTS = 2
+GROUP = 4
 
 
 def pack_kernel(owners, bricks, *rest, parts):
@@ -34,28 +34,31 @@
 
     lax.fori_loop(0, ndev, clear, 0)
 
-    def rank(g, sizes):
+    for i in range(parts):
+        slots[i] = 0
+
+    def rank(g, carry):
         d = owners[g]
         k = count[d]
         count[d] = k + 1
-        mine = k // part
-        grown = []
-        for i in range(parts):
-            listed[i * (nblk + 1) + sizes[i]] = g
-            slots[i * (nblk + 1) + sizes[i]] = d * part + k % part
-            grown.append(sizes[i] + jnp.where(mine == i, 1, 0))
-        return tuple(grown)
-
-    sizes = lax.fori_loop(0, nblk, rank, (0,) * parts)
+        mine = lax.div(k, part)
+        n = slots[mine]
+        slots[mine] = n + 1
+        listed[mine * nblk + n] = (d * part + (k - mine * part)) * nblk + g
+        return carry
+
+    lax.fori_loop(0, nblk, rank, 0)
     for copy in copies:
         copy.wait()
     for i, out in enumerate(outs):
-
-        def move(n, carry, i=i, out=out):
-            g = listed[i * (nblk + 1) + n]
-            at = slots[i * (nblk + 1) + n]
-            d = at // part
-            slot = pl.ds(at % part, 1)
+        size = slots[i]
+
+        def move(n, i=i, out=out):
+            item = listed[i * nblk + n]
+            at = lax.div(item, nblk)
+            g = item - at * nblk
+            d = lax.div(at, part)
+            slot = pl.ds(at - d * part, 1)
             row = pl.ds(g, 1)
             for j in range(3):
                 out[d, j, slot, :] = offsets[j, row, :]
@@ -65,9 +68,13 @@
                 out[d, 7 + j, slot, :] = affine[j, row, :]
             flat = cells[0, row, :] * 64 + cells[1, row, :] * 8 + cells[2, row, :]
             out[d, NCH - 1, slot, :] = (flat + bricks[g] * 512).astype(jnp.float32)
+
+        def moves(n, carry, size=size, move=move):
+            move(2 * n)
+            move(jnp.minimum(2 * n + 1, size - 1))
             return carry
 
-        lax.fori_loop(0, sizes[i], move, 0)
+        lax.fori_loop(0, lax.div(size + 1, 2), moves, 0)
 
 
 def halves(values):
@@ -108,11 +115,11 @@
 
     def block(n):
         s = chosen[n]
-        d = s // part
-        slot = pl.ds(s % part, 1)
-        brick = codes[s] // 512
-        uv = brick // (DEPTH // 8)
-        w = brick % (DEPTH // 8)
+        d = lax.div(s, part)
+        slot = pl.ds(s - d * part, 1)
+        brick = codes[s] >> 9
+        uv = lax.div(brick, DEPTH // 8)
+        w = lax.rem(brick, DEPTH // 8)
         ch = lambda j: moved[d, j, slot, :]
         flat = ch(NCH - 1).astype(jnp.int32) & 511
         cell_x = (flat >> 6).astype(jnp.float32)
@@ -245,8 +252,8 @@
             pltpu.VMEM((3, nblk, lanes), jnp.float32),
             pltpu.VMEM((9, nblk, lanes), jnp.float32),
             pltpu.SMEM((ndev,), jnp.int32),
-            pltpu.SMEM((parts * (nblk + 1),), jnp.int32),
-            pltpu.SMEM((parts * (nblk + 1),), jnp.int32),
+            pltpu.SMEM((parts * nblk,), jnp.int32),
+            pltpu.SMEM((parts,), jnp.int32),
             pltpu.SemaphoreType.DMA((5,)),
         ],
         name="pack",

time: 140 us -> 112 us (0.80)
  the two profiles are of different devices: /device:TPU:17 before, /device:TPU:5 now
where the time goes in v4:
time: 112 us; the launch traced here: 110 us
  blocking collectives  34.6 us (31%)
  Pallas kernels  26.4 us (24%)
  starting transfers between devices  21.9 us (20%)
  waiting for transfers between devices  21.9 us (20%)
  local copies, waits for them, and re-layouts  3.35 us (3%)
  other arithmetic  1.24 us (1%)
    all_to_all x1, blocking collectives, local(): lax.all_to_all(p, ('gx', 'yz'), split_axis=0, concat_axis=0, tiled=True)  34.6 us
    ppermute x4, starting transfers between devices, passed_along(): return lax.ppermute(array, axis, pairs)  18.3 us
    pallas_call x2, Pallas kernels, local(): pl.pallas_call(functools.partial(tile_kernel, not sums), out_shape=jax.Sh...  15.4 us
    all_to_all x1, waiting for transfers between devices, local(): lax.all_to_all(p, ('gx', 'yz'), split_axis=0, concat_axis=0, tiled=True)  12.4 us
    ppermute x4, waiting for transfers between devices, passed_along(): return lax.ppermute(array, axis, pairs)  9.54 us
    pallas_call x1, Pallas kernels, local(): pl.pallas_call(functools.partial(pack_kernel, parts=parts), out_shape=[ja...  6.59 us
    pallas_call x1, Pallas kernels, local(): pl.pallas_call(place_kernel, out_shape=jax.ShapeDtypeStruct((4, SIDE + 2,...  3.6 us
    all_to_all x1, starting transfers between devices, local(): lax.all_to_all(p, ('gx', 'yz'), split_axis=0, concat_axis=0, tiled=True)  3.52 us
  transfers between devices with their start and end apart: 5, of which 3 were waited for; matrix products, arithmetic and copies ran while one was open for 1% of the time, Pallas kernels for 12%

profile of v4, /device:TPU:5, one launch (start us, length us, event | category | flops | bytes accessed | tf_op | source)
XLA Modules:
  0.0 110.2 jit_solution(5726506940146280210)
XLA Ops:
  0.6 6.6 %pack.1 = (f32[32,17,4,128]{3,2,1,0:T(4,128)}, f32[32,17,4,128]{3,2,1,0:T(4,128)}) custom-call(s32[128]{0:T(128)} %bitcast.37, s32[128]{0:T(128)} %bricks.1, s32[3,128,128]{2,1,0:T(8,128)} %bitcast.32, f32[3,128,128]{2,1,0:T(8,128)} %bitcast.33, f32[128,128]{1,0:T(8,128)} %rest_2_.1, f32[3,128,128]{2,1,0:T(8,128)} %bitcast.34, f32[9,128,128]{2,1,0:T(8,128)} %bitcast.31), custom_call_target="tpu_custom_call" | custom-call | tf_op jit(solution)/shard_map/pack/pallas_call | solution.py:243
  7.2 34.6 %all_to_all.10.moved = f32[32,17,4,128]{3,2,1,0:T(4,128)S(1)} all-to-all(f32[32,17,4,128]{3,2,1,0:T(4,128)} %get-tuple-element.55), channel_id=1, replica_groups=mesh['gx'=4,'yz'=8] {'gx','yz'}, dimensions={0} | all-to-all | bytes 2228224 | tf_op jit(solution)/shard_map/all_to_all | solution.py:273
  41.9 3.5 %all-to-all-start.1 = ((f32[32,17,4,128]{3,2,1,0:T(4,128)}), f32[32,17,4,128]{3,2,1,0:T(4,128)S(1)}, u32[]{:S(2)}, u32[]{:S(2)}) async-start(f32[32,17,4,128]{3,2,1,0:T(4,128)} %get-tuple-element.56), calls=%async_computation.1 | async-start | bytes 2228224 | tf_op jit(solution)/shard_map/all_to_all | solution.py:273
  45.4 0.6 convert_reduce_fusion
  46.0 0.1 convert_element_type.17.codes
  46.1 13.6 %tiles.2.rest_0_ = f32[16,4,64,128]{3,2,1,0:T(8,128)S(1)} custom-call(s32[128]{0:T(128)S(1)} %convert_element_type.17.codes, f32[32,17,4,128]{3,2,1,0:T(4,128)S(1)} %all_to_all.10.moved), custom_call_target="tpu_custom_call" | custom-call | flops 20000000000 | bytes 4000000 | tf_op jit(solution)/shard_map/tiles/pallas_call | solution.py:278
  59.7 0.0 copy-start
  59.7 1.3 %copy-done = f32[16,4,64,128]{3,2,1,0:T(8,128)} copy-done((f32[16,4,64,128]{3,2,1,0:T(8,128)}, f32[16,4,64,128]{3,2,1,0:T(8,128)S(1)}, u32[]{:S(2)}) %copy-start) | copy-done | bytes 2097176
  61.0 12.4 %all-to-all-done.1.moved = f32[32,17,4,128]{3,2,1,0:T(4,128)S(1)} async-done(((f32[32,17,4,128]{3,2,1,0:T(4,128)}), f32[32,17,4,128]{3,2,1,0:T(4,128)S(1)}, u32[]{:S(2)}, u32[]{:S(2)}) %all-to-all-start.1) | async-done | bytes 1114144 | tf_op jit(solution)/shard_map/all_to_all | solution.py:273
  73.4 0.6 fusion
  74.0 0.1 convert_element_type.15.codes
  74.1 0.0 copy-start.1
  74.2 1.6 %copy-done.1 = f32[16,4,64,128]{3,2,1,0:T(8,128)S(1)} copy-done((f32[16,4,64,128]{3,2,1,0:T(8,128)S(1)}, f32[16,4,64,128]{3,2,1,0:T(8,128)}, u32[]{:S(2)}) %copy-start.1) | copy-done | bytes 2097176
  75.7 1.8 %tiles.3.acc = f32[16,4,64,128]{3,2,1,0:T(8,128)S(1)} custom-call(s32[128]{0:T(128)S(1)} %convert_element_type.15.codes, f32[32,17,4,128]{3,2,1,0:T(4,128)S(1)} %all-to-all-done.1.moved, f32[16,4,64,128]{3,2,1,0:T(8,128)S(1)} %copy-done.1), custom_call_target="tpu_custom_call" | custom-call | flops 20000000000 | bytes 4000000 | tf_op jit(solution)/shard_map/tiles/pallas_call | solution.py:278
  77.5 3.6 %place.1.grid = f32[4,18,18,128]{3,2,1,0:T(8,128)S(1)} custom-call(f32[16,4,64,128]{3,2,1,0:T(8,128)S(1)} %tiles.3.acc), custom_call_target="tpu_custom_call" | custom-call | tf_op jit(solution)/shard_map/place/pallas_call | solution.py:291
  81.2 2.4 %collective-permute-start = (f32[4,18,128]{2,1,0:T(8,128)S(1)}, f32[4,18,128]{2,1,0:T(8,128)S(1)}, u32[]{:S(2)}, u32[]{:S(2)}) collective-permute-start(f32[4,18,128]{2,1,0:T(8,128)S(1)} %get-tuple-element.63), channel_id=1, source_target_pairs={{0,8},{8,16},{16,24},{1,9},{9,17},{17,25},{2,10},{10,18},{18,26},{... | collective-permute-start | bytes 110600 | tf_op jit(solution)/shard_map/ppermute | solution.py:228
  83.6 1.9 %collective-permute-start.1 = (f32[4,18,128]{2,1,0:T(8,128)S(1)}, f32[4,18,128]{2,1,0:T(8,128)S(1)}, u32[]{:S(2)}, u32[]{:S(2)}) collective-permute-start(f32[4,18,128]{2,1,0:T(8,128)S(1)} %get-tuple-element.62), channel_id=1, source_target_pairs={{8,0},{16,8},{24,16},{9,1},{17,9},{25,17},{10,2},{18,10},{26,18},{... | collective-permute-start | bytes 110600 | tf_op jit(solution)/shard_map/ppermute | solution.py:228
  85.6 0.0 collective-permute-done.xlow
  85.7 3.8 %collective-permute-done.1.xhigh = f32[4,18,128]{2,1,0:T(8,128)S(1)} collective-permute-done((f32[4,18,128]{2,1,0:T(8,128)S(1)}, f32[4,18,128]{2,1,0:T(8,128)S(1)}, u32[]{:S(2)}, u32[]{:S(2)}) %collective-permute-start.1) | collective-permute-done | bytes 36896 | tf_op jit(solution)/shard_map/ppermute | solution.py:228
  89.5 4.2 %collective-permute-start.2 = (f32[4,16,128]{2,1,0:T(8,128)S(1)}, f32[4,16,128]{2,1,0:T(8,128)S(1)}, u32[]{:S(2)}, u32[]{:S(2)}) collective-permute-start(f32[4,16,128]{2,1,0:T(8,128)S(1)} %scatter-add.15), channel_id=1, source_target_pairs={{0,1},{1,2},{2,3},{3,4},{4,5},{5,6},{6,7},{8,9},{9,10},{10,11},{11... | collective-permute-start | bytes 98312 | tf_op jit(solution)/shard_map/ppermute | solution.py:228
  93.8 9.8 %collective-permute-start.3 = (f32[4,16,128]{2,1,0:T(8,128)S(1)}, f32[4,16,128]{2,1,0:T(8,128)S(1)}, u32[]{:S(2)}, u32[]{:S(2)}) collective-permute-start(f32[4,16,128]{2,1,0:T(8,128)S(1)} %scatter-add.19), channel_id=1, source_target_pairs={{1,0},{2,1},{3,2},{4,3},{5,4},{6,5},{7,6},{9,8},{10,9},{11,10},{12... | collective-permute-start | bytes 98312 | tf_op jit(solution)/shard_map/ppermute | solution.py:228
  103.6 0.0 collective-permute-done.2.ylow
  103.6 5.8 %collective-permute-done.3.yhigh = f32[4,16,128]{2,1,0:T(8,128)S(1)} collective-permute-done((f32[4,16,128]{2,1,0:T(8,128)S(1)}, f32[4,16,128]{2,1,0:T(8,128)S(1)}, u32[]{:S(2)}, u32[]{:S(2)}) %collective-permute-start.3) | collective-permute-done | bytes 32800 | tf_op jit(solution)/shard_map/ppermute | solution.py:228
  109.3 0.9 finish.1
  (8 shorter events, 0.2 us)
Async XLA Ops:
  41.9 31.5 %all-to-all-start.1 = ((f32[32,17,4,128]{3,2,1,0:T(4,128)}), f32[32,17,4,128]{3,2,1,0:T(4,128)S(1)}, u32[]{:S(2)}, u32[]{:S(2)}) async-start(f32[32,17,4,128]{3,2,1,0:T(4,128)} %get-tuple-element.56), calls=%async_computation.1 | async-start | bytes 2228224 | tf_op jit(solution)/shard_map/all_to_all | solution.py:273
  59.7 1.3 %copy-start = (f32[16,4,64,128]{3,2,1,0:T(8,128)}, f32[16,4,64,128]{3,2,1,0:T(8,128)S(1)}, u32[]{:S(2)}) copy-start(f32[16,4,64,128]{3,2,1,0:T(8,128)S(1)} %tiles.2.rest_0_) | copy-start | bytes 6291460
  74.1 1.6 %copy-start.1 = (f32[16,4,64,128]{3,2,1,0:T(8,128)S(1)}, f32[16,4,64,128]{3,2,1,0:T(8,128)}, u32[]{:S(2)}) copy-start(f32[16,4,64,128]{3,2,1,0:T(8,128)} %copy-done) | copy-start | bytes 6291460
  81.2 4.4 %collective-permute-start = (f32[4,18,128]{2,1,0:T(8,128)S(1)}, f32[4,18,128]{2,1,0:T(8,128)S(1)}, u32[]{:S(2)}, u32[]{:S(2)}) collective-permute-start(f32[4,18,128]{2,1,0:T(8,128)S(1)} %get-tuple-element.63), channel_id=1, source_target_pairs={{0,8},{8,16},{16,24},{1,9},{9,17},{17,25},{2,10},{10,18},{18,26},{... | collective-permute-start | bytes 110600 | tf_op jit(solution)/shard_map/ppermute | solution.py:228
  83.6 5.8 %collective-permute-start.1 = (f32[4,18,128]{2,1,0:T(8,128)S(1)}, f32[4,18,128]{2,1,0:T(8,128)S(1)}, u32[]{:S(2)}, u32[]{:S(2)}) collective-permute-start(f32[4,18,128]{2,1,0:T(8,128)S(1)} %get-tuple-element.62), channel_id=1, source_target_pairs={{8,0},{16,8},{24,16},{9,1},{17,9},{25,17},{10,2},{18,10},{26,18},{... | collective-permute-start | bytes 110600 | tf_op jit(solution)/shard_map/ppermute | solution.py:228
  89.5 14.0 %collective-permute-start.2 = (f32[4,16,128]{2,1,0:T(8,128)S(1)}, f32[4,16,128]{2,1,0:T(8,128)S(1)}, u32[]{:S(2)}, u32[]{:S(2)}) collective-permute-start(f32[4,16,128]{2,1,0:T(8,128)S(1)} %scatter-add.15), channel_id=1, source_target_pairs={{0,1},{1,2},{2,3},{3,4},{4,5},{5,6},{6,7},{8,9},{9,10},{10,11},{11... | collective-permute-start | bytes 98312 | tf_op jit(solution)/shard_map/ppermute | solution.py:228
  93.8 15.6 %collective-permute-start.3 = (f32[4,16,128]{2,1,0:T(8,128)S(1)}, f32[4,16,128]{2,1,0:T(8,128)S(1)}, u32[]{:S(2)}, u32[]{:S(2)}) collective-permute-start(f32[4,16,128]{2,1,0:T(8,128)S(1)} %scatter-add.19), channel_id=1, source_target_pairs={{1,0},{2,1},{3,2},{4,3},{5,4},{6,5},{7,6},{9,8},{10,9},{11,10},{12... | collective-permute-start | bytes 98312 | tf_op jit(solution)/shard_map/ppermute | solution.py:228

commit v5 on v4

--- a/solution.py
+++ b/solution.py
@@ -13,7 +13,7 @@
 NCH = 17
 NUV = 4
 PARTS = 2
-GROUP = 4
+GROUP = 8
 
 
 def pack_kernel(owners, bricks, *rest, parts):
@@ -190,6 +190,12 @@
                     grid[c, 8 * u + x, 8 * v : 8 * v + 10, :] += put[
                         base : base + 10, i * DEPTH : (i + 1) * DEPTH
                     ]
+
+
+def last_kernel(first, codes, moved, *rest):
+    grid, acc, chosen, wide, key = rest[-5:]
+    tile_kernel(first, codes, moved, *rest[:-5], acc, chosen)
+    place_kernel(acc, grid, wide, key)
 
 
 def finish_kernel(grid, xlow, xhigh, ylow, yhigh, mass, speed):
@@ -271,35 +277,34 @@
         if moved:
             p, moved[-1] = lax.optimization_barrier((p, moved[-1]))
         moved.append(lax.all_to_all(p, ("gx", "yz"), split_axis=0, concat_axis=0, tiled=True))
+    held = (DEPTH // 8, NUV, 64, DEPTH)
     sums = []
-    for arrived in moved:
+    for i, arrived in enumerate(moved):
         codes = arrived[:, NCH - 1, :, 0].astype(jnp.int32).reshape(ndev * part)
+        last = i == parts - 1
+        chosen = pltpu.SMEM((ndev * part + 1,), jnp.int32)
+        scratch = [
+            pltpu.VMEM(held, jnp.float32),
+            chosen,
+            pltpu.VMEM((2 * NUV * 64, (DEPTH // 8) * DEPTH), jnp.bfloat16),
+            pltpu.VMEM(((DEPTH // 8) * DEPTH, DEPTH), jnp.int32),
+        ]
+        shape = (4, SIDE + 2, SIDE + 2, DEPTH) if last else held
         sums = [
             pl.pallas_call(
-                functools.partial(tile_kernel, not sums),
-                out_shape=jax.ShapeDtypeStruct((DEPTH // 8, NUV, 64, DEPTH), jnp.float32),
+                functools.partial(last_kernel if last else tile_kernel, not sums),
+                out_shape=jax.ShapeDtypeStruct(shape, jnp.float32),
                 in_specs=[SMEM, VMEM] + [VMEM] * len(sums),
                 out_specs=VMEM,
-                scratch_shapes=[pltpu.SMEM((ndev * part + 1,), jnp.int32)],
+                scratch_shapes=scratch if last else [chosen],
                 compiler_params=PARAMS,
                 cost_estimate=pl.CostEstimate(
                     flops=40_000_000_000 // parts, bytes_accessed=4_000_000, transcendentals=0
                 ),
-                name="tiles",
+                name="last_tiles" if last else "tiles",
             )(codes, arrived, *sums)
         ]
-    grid = pl.pallas_call(
-        place_kernel,
-        out_shape=jax.ShapeDtypeStruct((4, SIDE + 2, SIDE + 2, DEPTH), jnp.float32),
-        in_specs=[VMEM],
-        out_specs=VMEM,
-        scratch_shapes=[
-            pltpu.VMEM((2 * NUV * 64, (DEPTH // 8) * DEPTH), jnp.bfloat16),
-            pltpu.VMEM(((DEPTH // 8) * DEPTH, DEPTH), jnp.int32),
-        ],
-        compiler_params=PARAMS,
-        name="place",
-    )(*sums)
+    grid = sums[0]
     xlow = passed_along(grid[:, SIDE + 1], "gx", 1)
     xhigh = passed_along(grid[:, 0], "gx", -1)
 

time: 112 us -> 110 us (0.982)
  the two profiles are of different devices: /device:TPU:5 before, /device:TPU:21 now
where the time goes in v5:
time: 110 us; the launch traced here: 109 us
  blocking collectives  32.6 us (30%)
  starting transfers between devices  28.7 us (26%)
  Pallas kernels  28.5 us (26%)
  waiting for transfers between devices  14.2 us (13%)
  local copies, waits for them, and re-layouts  3.35 us (3%)
  other arithmetic  1.24 us (1%)
    all_to_all x1, blocking collectives, local(): lax.all_to_all(p, ('gx', 'yz'), split_axis=0, concat_axis=0, tiled=True)  32.6 us
    ppermute x4, starting transfers between devices, passed_along(): return lax.ppermute(array, axis, pairs)  23.2 us
    pallas_call x2, Pallas kernels, local(): pl.pallas_call(functools.partial(last_kernel if last else tile_kernel, no...  21 us
    all_to_all x1, waiting for transfers between devices, local(): lax.all_to_all(p, ('gx', 'yz'), split_axis=0, concat_axis=0, tiled=True)  8.27 us
    pallas_call x1, Pallas kernels, local(): pl.pallas_call(functools.partial(pack_kernel, parts=parts), out_shape=[ja...  6.59 us
    ppermute x4, waiting for transfers between devices, passed_along(): return lax.ppermute(array, axis, pairs)  5.92 us
    all_to_all x1, starting transfers between devices, local(): lax.all_to_all(p, ('gx', 'yz'), split_axis=0, concat_axis=0, tiled=True)  5.48 us
    unnamed x4, local copies, waits for them, and re-layouts  2.93 us
  transfers between devices with their start and end apart: 5, of which 3 were waited for; matrix products, arithmetic and copies ran while one was open for 1% of the time, Pallas kernels for 14%

profile of v5, /device:TPU:21, one launch (start us, length us, event | category | flops | bytes accessed | tf_op | source)
XLA Modules:
  0.0 109.3 jit_solution(1757922466445438195)
XLA Ops:
  0.6 6.6 %pack.1 = (f32[32,17,4,128]{3,2,1,0:T(4,128)}, f32[32,17,4,128]{3,2,1,0:T(4,128)}) custom-call(s32[128]{0:T(128)} %bitcast.37, s32[128]{0:T(128)} %bricks.1, s32[3,128,128]{2,1,0:T(8,128)} %bitcast.32, f32[3,128,128]{2,1,0:T(8,128)} %bitcast.33, f32[128,128]{1,0:T(8,128)} %rest_2_.1, f32[3,128,128]{2,1,0:T(8,128)} %bitcast.34, f32[9,128,128]{2,1,0:T(8,128)} %bitcast.31), custom_call_target="tpu_custom_call" | custom-call | tf_op jit(solution)/shard_map/pack/pallas_call | solution.py:249
  7.2 32.6 %all_to_all.10.moved = f32[32,17,4,128]{3,2,1,0:T(4,128)S(1)} all-to-all(f32[32,17,4,128]{3,2,1,0:T(4,128)} %get-tuple-element.55), channel_id=1, replica_groups=mesh['gx'=4,'yz'=8] {'gx','yz'}, dimensions={0} | all-to-all | bytes 2228224 | tf_op jit(solution)/shard_map/all_to_all | solution.py:279
  39.8 5.5 %all-to-all-start.1 = ((f32[32,17,4,128]{3,2,1,0:T(4,128)}), f32[32,17,4,128]{3,2,1,0:T(4,128)S(1)}, u32[]{:S(2)}, u32[]{:S(2)}) async-start(f32[32,17,4,128]{3,2,1,0:T(4,128)} %get-tuple-element.56), calls=%async_computation.1 | async-start | bytes 2228224 | tf_op jit(solution)/shard_map/all_to_all | solution.py:279
  45.3 0.6 convert_reduce_fusion
  45.9 0.1 convert_element_type.17.codes
  46.0 14.9 %tiles.1.rest_0_ = f32[16,4,64,128]{3,2,1,0:T(8,128)S(1)} custom-call(s32[128]{0:T(128)S(1)} %convert_element_type.17.codes, f32[32,17,4,128]{3,2,1,0:T(4,128)S(1)} %all_to_all.10.moved), custom_call_target="tpu_custom_call" | custom-call | flops 20000000000 | bytes 4000000 | tf_op jit(solution)/shard_map/tiles/pallas_call | solution.py:294
  61.0 0.0 copy-start
  61.0 1.3 %copy-done = f32[16,4,64,128]{3,2,1,0:T(8,128)} copy-done((f32[16,4,64,128]{3,2,1,0:T(8,128)}, f32[16,4,64,128]{3,2,1,0:T(8,128)S(1)}, u32[]{:S(2)}) %copy-start) | copy-done | bytes 2097176
  62.3 8.3 %all-to-all-done.1.moved = f32[32,17,4,128]{3,2,1,0:T(4,128)S(1)} async-done(((f32[32,17,4,128]{3,2,1,0:T(4,128)}), f32[32,17,4,128]{3,2,1,0:T(4,128)S(1)}, u32[]{:S(2)}, u32[]{:S(2)}) %all-to-all-start.1) | async-done | bytes 1114144 | tf_op jit(solution)/shard_map/all_to_all | solution.py:279
  70.6 0.6 fusion
  71.2 0.1 convert_element_type.15.codes
  71.3 0.0 copy-start.1
  71.3 1.6 %copy-done.1 = f32[16,4,64,128]{3,2,1,0:T(8,128)S(1)} copy-done((f32[16,4,64,128]{3,2,1,0:T(8,128)S(1)}, f32[16,4,64,128]{3,2,1,0:T(8,128)}, u32[]{:S(2)}) %copy-start.1) | copy-done | bytes 2097176
  72.9 6.1 %last_tiles.1.grid = f32[4,18,18,128]{3,2,1,0:T(8,128)S(1)} custom-call(s32[128]{0:T(128)S(1)} %convert_element_type.15.codes, f32[32,17,4,128]{3,2,1,0:T(4,128)S(1)} %all-to-all-done.1.moved, f32[16,4,64,128]{3,2,1,0:T(8,128)S(1)} %copy-done.1), custom_call_target="tpu_custom_call" | custom-call | flops 20000000000 | bytes 4000000 | tf_op jit(solution)/shard_map/last_tiles/pallas_call | solution.py:294
  79.0 2.9 %collective-permute-start = (f32[4,18,128]{2,1,0:T(8,128)S(1)}, f32[4,18,128]{2,1,0:T(8,128)S(1)}, u32[]{:S(2)}, u32[]{:S(2)}) collective-permute-start(f32[4,18,128]{2,1,0:T(8,128)S(1)} %get-tuple-element.63), channel_id=1, source_target_pairs={{0,8},{8,16},{16,24},{1,9},{9,17},{17,25},{2,10},{10,18},{18,26},{... | collective-permute-start | bytes 110600 | tf_op jit(solution)/shard_map/ppermute | solution.py:234
  82.0 3.0 %collective-permute-start.1 = (f32[4,18,128]{2,1,0:T(8,128)S(1)}, f32[4,18,128]{2,1,0:T(8,128)S(1)}, u32[]{:S(2)}, u32[]{:S(2)}) collective-permute-start(f32[4,18,128]{2,1,0:T(8,128)S(1)} %get-tuple-element.62), channel_id=1, source_target_pairs={{8,0},{16,8},{24,16},{9,1},{17,9},{25,17},{10,2},{18,10},{26,18},{... | collective-permute-start | bytes 110600 | tf_op jit(solution)/shard_map/ppermute | solution.py:234
  85.0 0.0 collective-permute-done.xlow
  85.1 2.3 %collective-permute-done.1.xhigh = f32[4,18,128]{2,1,0:T(8,128)S(1)} collective-permute-done((f32[4,18,128]{2,1,0:T(8,128)S(1)}, f32[4,18,128]{2,1,0:T(8,128)S(1)}, u32[]{:S(2)}, u32[]{:S(2)}) %collective-permute-start.1) | collective-permute-done | bytes 36896 | tf_op jit(solution)/shard_map/ppermute | solution.py:234
  87.5 15.3 %collective-permute-start.2 = (f32[4,16,128]{2,1,0:T(8,128)S(1)}, f32[4,16,128]{2,1,0:T(8,128)S(1)}, u32[]{:S(2)}, u32[]{:S(2)}) collective-permute-start(f32[4,16,128]{2,1,0:T(8,128)S(1)} %scatter-add.15), channel_id=1, source_target_pairs={{0,1},{1,2},{2,3},{3,4},{4,5},{5,6},{6,7},{8,9},{9,10},{10,11},{11... | collective-permute-start | bytes 98312 | tf_op jit(solution)/shard_map/ppermute | solution.py:234
  102.9 1.9 %collective-permute-start.3 = (f32[4,16,128]{2,1,0:T(8,128)S(1)}, f32[4,16,128]{2,1,0:T(8,128)S(1)}, u32[]{:S(2)}, u32[]{:S(2)}) collective-permute-start(f32[4,16,128]{2,1,0:T(8,128)S(1)} %scatter-add.19), channel_id=1, source_target_pairs={{1,0},{2,1},{3,2},{4,3},{5,4},{6,5},{7,6},{9,8},{10,9},{11,10},{12... | collective-permute-start | bytes 98312 | tf_op jit(solution)/shard_map/ppermute | solution.py:234
  104.8 0.0 collective-permute-done.2.ylow
  104.8 3.6 %collective-permute-done.3.yhigh = f32[4,16,128]{2,1,0:T(8,128)S(1)} collective-permute-done((f32[4,16,128]{2,1,0:T(8,128)S(1)}, f32[4,16,128]{2,1,0:T(8,128)S(1)}, u32[]{:S(2)}, u32[]{:S(2)}) %collective-permute-start.3) | collective-permute-done | bytes 32800 | tf_op jit(solution)/shard_map/ppermute | solution.py:234
  108.4 0.9 finish.1
  (8 shorter events, 0.2 us)
Async XLA Ops:
  39.8 30.8 %all-to-all-start.1 = ((f32[32,17,4,128]{3,2,1,0:T(4,128)}), f32[32,17,4,128]{3,2,1,0:T(4,128)S(1)}, u32[]{:S(2)}, u32[]{:S(2)}) async-start(f32[32,17,4,128]{3,2,1,0:T(4,128)} %get-tuple-element.56), calls=%async_computation.1 | async-start | bytes 2228224 | tf_op jit(solution)/shard_map/all_to_all | solution.py:279
  61.0 1.3 %copy-start = (f32[16,4,64,128]{3,2,1,0:T(8,128)}, f32[16,4,64,128]{3,2,1,0:T(8,128)S(1)}, u32[]{:S(2)}) copy-start(f32[16,4,64,128]{3,2,1,0:T(8,128)S(1)} %tiles.1.rest_0_) | copy-start | bytes 6291460
  71.3 1.6 %copy-start.1 = (f32[16,4,64,128]{3,2,1,0:T(8,128)S(1)}, f32[16,4,64,128]{3,2,1,0:T(8,128)}, u32[]{:S(2)}) copy-start(f32[16,4,64,128]{3,2,1,0:T(8,128)} %copy-done) | copy-start | bytes 6291460
  79.0 6.0 %collective-permute-start = (f32[4,18,128]{2,1,0:T(8,128)S(1)}, f32[4,18,128]{2,1,0:T(8,128)S(1)}, u32[]{:S(2)}, u32[]{:S(2)}) collective-permute-start(f32[4,18,128]{2,1,0:T(8,128)S(1)} %get-tuple-element.63), channel_id=1, source_target_pairs={{0,8},{8,16},{16,24},{1,9},{9,17},{17,25},{2,10},{10,18},{18,26},{... | collective-permute-start | bytes 110600 | tf_op jit(solution)/shard_map/ppermute | solution.py:234
  82.0 5.4 %collective-permute-start.1 = (f32[4,18,128]{2,1,0:T(8,128)S(1)}, f32[4,18,128]{2,1,0:T(8,128)S(1)}, u32[]{:S(2)}, u32[]{:S(2)}) collective-permute-start(f32[4,18,128]{2,1,0:T(8,128)S(1)} %get-tuple-element.62), channel_id=1, source_target_pairs={{8,0},{16,8},{24,16},{9,1},{17,9},{25,17},{10,2},{18,10},{26,18},{... | collective-permute-start | bytes 110600 | tf_op jit(solution)/shard_map/ppermute | solution.py:234
  87.5 17.3 %collective-permute-start.2 = (f32[4,16,128]{2,1,0:T(8,128)S(1)}, f32[4,16,128]{2,1,0:T(8,128)S(1)}, u32[]{:S(2)}, u32[]{:S(2)}) collective-permute-start(f32[4,16,128]{2,1,0:T(8,128)S(1)} %scatter-add.15), channel_id=1, source_target_pairs={{0,1},{1,2},{2,3},{3,4},{4,5},{5,6},{6,7},{8,9},{9,10},{10,11},{11... | collective-permute-start | bytes 98312 | tf_op jit(solution)/shard_map/ppermute | solution.py:234
  102.9 5.6 %collective-permute-start.3 = (f32[4,16,128]{2,1,0:T(8,128)S(1)}, f32[4,16,128]{2,1,0:T(8,128)S(1)}, u32[]{:S(2)}, u32[]{:S(2)}) collective-permute-start(f32[4,16,128]{2,1,0:T(8,128)S(1)} %scatter-add.19), channel_id=1, source_target_pairs={{1,0},{2,1},{3,2},{4,3},{5,4},{6,5},{7,6},{9,8},{10,9},{11,10},{12... | collective-permute-start | bytes 98312 | tf_op jit(solution)/shard_map/ppermute | solution.py:234
